TPU v7x, 128 devices: a whole 4x4x4 slice. The times are simulated.
128 devices in a mesh: prow: 8 (over y, z_hi), pcol: 16 (over z_lo, x, core).
Axes of the slice: x: 4, y: 4, z: 4 (z_hi: 2, z_lo: 2; z = z_hi * 2 + z_lo), core: 2. Of those that a mesh axis runs over, the one named last changes fastest.
Arguments:
- factors: bfloat16 [8, 2048, 1024], P('prow', 'pcol'), may hold values from -0.1875 to 0.1875
- shift: float32 [8, 2048], P('prow'), may hold values from 0.5 to 4
Outputs:
- factored: float32 [8, 2048, 16, 1024], P('prow', None, 'pcol')
All inputs are finite; a program needn't handle non-finite values.
Results may differ from a plain program's by a relative error of at most 0.0003.
Values may be sent and summed in bfloat16 or wider, within the bound.
No kernel may reach another device: no remote copies, remote signals or barrier semaphores. Data moves between devices by JAX's collectives and lax.ppermute only.
A program may use at most 128 MiB of HBM per device.

v0:
```python
import jax
import jax.numpy as jnp
from jax import lax
from jax.sharding import PartitionSpec as P

NB = 256
TC = 4


def from_root(array, axis, root):
    mine = lax.axis_index(axis) == root
    return lax.psum(jnp.where(mine, array, jnp.zeros_like(array)), axis)


def local(factors, shift):
    nprow = lax.axis_size("prow")
    npcol = lax.axis_size("pcol")
    prow_index = lax.axis_index("prow")
    pcol_index = lax.axis_index("pcol")
    owned_rows = factors[0]
    row_count = owned_rows.shape[0]
    owner_len = shift.shape[1]
    tile_rows = owner_len // NB
    width = TC * NB
    col_ratio = npcol // nprow
    contract = (((1,), (1,)), ((), ()))
    schur_rows = lax.dot_general(
        owned_rows,
        lax.all_gather(factors, ("prow", "pcol"), axis=1, tiled=True)[0],
        contract,
        preferred_element_type=jnp.float32,
    )
    schur_rows = schur_rows.reshape(row_count, nprow, tile_rows, NB).transpose(0, 2, 1, 3)
    schur_rows = schur_rows.reshape(row_count, TC, npcol, NB)
    moved = lax.all_to_all(schur_rows, "pcol", split_axis=2, concat_axis=0, tiled=True)
    block = moved.reshape(owner_len, width)
    row_local = jnp.arange(owner_len, dtype=jnp.int32)
    col_local = jnp.arange(width, dtype=jnp.int32)
    row_global = (row_local // NB * nprow + prow_index) * NB + row_local % NB
    col_global = (col_local // NB * npcol + pcol_index) * NB + col_local % NB
    block = block + jnp.where(
        row_global[:, None] == col_global[None, :], shift[0][:, None], jnp.float32(0.0)
    )
    corner_tile = from_root(block[:NB, :NB], "prow", 0)
    identity = jnp.eye(NB, dtype=jnp.float32)
    corner_tile = jnp.where(pcol_index == 0, corner_tile, identity)
    diagonal_factor = jnp.linalg.cholesky(corner_tile)
    column = block[:, :NB]
    panel = lax.linalg.triangular_solve(
        diagonal_factor, column, left_side=False, lower=True, transpose_a=True
    )
    first_rows = (prow_index == 0) & (row_local < NB)
    padded_factor = jnp.pad(diagonal_factor, ((0, owner_len - NB), (0, 0)))
    panel = jnp.where(first_rows[:, None], padded_factor, panel)
    panel_here = from_root(panel, "pcol", 0)
    chosen = lax.dynamic_slice_in_dim(
        panel_here.reshape(TC, col_ratio, NB, NB), pcol_index // nprow, 1, 1
    )
    panel_there = from_root(chosen.reshape(width, NB), "prow", pcol_index % nprow)
    updated = block - jnp.dot(panel_here, panel_there.T, precision=lax.Precision.HIGHEST)
    updated = jnp.where(first_rows[:, None], block, updated)
    first_cols = (pcol_index == 0) & (col_local < NB)
    panel_wide = jnp.pad(panel_here, ((0, 0), (0, width - NB)))
    updated = jnp.where(first_cols[None, :], panel_wide, updated)
    return updated[None, :, None, :]


def solution(mesh):
    in_specs = (P("prow", "pcol", None), P("prow", None))
    out_specs = P("prow", None, "pcol", None)
    return jax.shard_map(local, mesh=mesh, in_specs=in_specs, out_specs=out_specs, check_vma=False)
```

profile of v0, /device:TPU:1, one launch (start us, length us, event | category | flops | bytes accessed | tf_op | source)
XLA Modules:
  0.0 714.8 jit_solution(10315444625872561178)
XLA Ops:
  7.3 113.5 %all-gather.2.cloned.1.call-done = bf16[1,16384,1024]{2,1,0:T(8,128)(2,1)} async-done(((bf16[1,128,1024]{2,1,0:T(8,128)(2,1)}), bf16[1,16384,1024]{2,1,0:T(8,128)(2,1)}) %all-gather.2.cloned.1.call-update) | async-done | bytes 33554448 | tf_op jit(solution)/shard_map/all_gather | solution.py:29
  120.8 19.3 %convolution_bitcast_fusion = f32[128,8,8,256]{3,0,1,2:T(8,128)} fusion(bf16[8,8,256,1024]{3,2,1,0:T(8,128)(2,1)} %bitcast.59, bf16[1,128,1024]{2,1,0:T(8,128)(2,1)} %param.2), kind=kOutput, calls=%fused_computation.6 | convolution fusion | flops 4294967296 | bytes 42205184 | tf_op jit(solution)/shard_map/dot_general | solution.py:27
  140.1 11.5 %copy.19 = f32[128,8,8,256]{3,2,1,0:T(8,128)} copy(f32[128,8,8,256]{3,0,1,2:T(8,128)} %convolution_bitcast_fusion) | data formatting | bytes 16777216 | tf_op jit(solution)/shard_map/transpose | solution.py:33
  151.5 12.2 %copy.20 = f32[128,4,16,256]{3,1,0,2:T(4,128)} copy(f32[128,4,16,256]{3,2,1,0:T(8,128)} %bitcast.60) | data formatting | bytes 16777216 | tf_op jit(solution)/shard_map/reshape | solution.py:34
  163.7 4.7 all-to-all-start
  168.4 10.0 %all-reduce.7.cloned.1.call-start = ((), (), s32[]{:S(2)}) async-start(), calls=%async_computation.2 | async-start | bytes 524288 | tf_op jit(solution)/shard_map/psum | solution.py:12
  178.5 102.3 %all-to-all-done = f32[128,4,16,256]{3,1,0,2:T(4,128)} async-done(((f32[128,4,16,256]{3,1,0,2:T(4,128)}), f32[128,4,16,256]{3,1,0,2:T(4,128)}, u32[]{:S(2)}, u32[]{:S(2)}) %all-to-all-start) | async-done | bytes 8388640 | tf_op jit(solution)/shard_map/all_to_all | solution.py:35
  280.8 8.9 %copy.35 = f32[256,8,4,256]{3,1,2,0:T(8,128)} copy(f32[256,8,4,256]{3,2,1,0:T(4,128)} %bitcast.23) | data formatting | bytes 16777216
  289.7 9.2 %copy.33 = f32[2048,1024]{0,1:T(8,128)} copy(f32[2048,1024]{1,0:T(8,128)} %bitcast.61) | data formatting | bytes 16777216 | tf_op jit(solution)/shard_map/reshape | solution.py:36
  298.8 4.1 select_add_fusion
  303.0 3.4 copy-done
  307.2 78.6 %all-reduce.7.cloned.1.call-done = f32[256,256]{0,1:T(8,128)} async-done(((f32[256,256]{0,1:T(8,128)}), f32[256,256]{0,1:T(8,128)}) %all-reduce.7.cloned.1.call-update) | async-done | bytes 262160 | tf_op jit(solution)/shard_map/psum | solution.py:12
  386.0 11.7 %cholesky.49 = f32[128,128]{1,0:T(8,128)S(1)} custom-call(f32[128,128]{1,0:T(8,128)S(1)} %cholesky.115), custom_call_target="Cholesky" | custom-call | tf_op jit(solution)/shard_map/jit(cholesky)/cholesky | solution.py:47
  397.9 9.8 %custom-call.14 = f32[1,128,128]{1,2,0:T(8,128)S(1)} custom-call(f32[1,128,128]{2,1,0:T(8,128)S(1)} %get-tuple-element.38), custom_call_target="InvertDiagBlocksLowerTriangular" | custom-call | tf_op jit(solution)/shard_map/jit(cholesky)/cholesky | solution.py:47
  408.3 11.7 %cholesky.103 = f32[128,128]{1,0:T(8,128)S(1)} custom-call(f32[128,128]{1,0:T(8,128)S(1)} %convolution_subtract_fusion.1), custom_call_target="Cholesky" | custom-call | tf_op jit(solution)/shard_map/jit(cholesky)/cholesky | solution.py:47
  422.3 4.5 while.1
  426.8 19.7 %custom-call.15 = f32[2,128,128]{1,2,0:T(8,128)S(1)} custom-call(f32[2,128,128]{2,1,0:T(8,128)S(1)} %get-tuple-element.12), custom_call_target="InvertDiagBlocksLowerTriangular" | custom-call | tf_op jit(solution)/shard_map/triangular_solve | solution.py:49
  448.7 2.3 convolution_subtract_fusion
  453.8 125.6 %all-reduce.9.cloned.1.call-done = f32[2048,256]{0,1:T(8,128)} async-done(((f32[2048,256]{0,1:T(8,128)}), f32[2048,256]{0,1:T(8,128)}) %all-reduce.9.cloned.1.call-update) | async-done | bytes 2097168 | tf_op jit(solution)/shard_map/psum | solution.py:12
  579.4 4.3 reshape.95
  583.8 5.0 fusion.3
  589.9 85.4 %all-reduce.11.cloned.1.call-done = f32[1024,256]{0,1:T(8,128)} async-done(((f32[1024,256]{0,1:T(8,128)}), f32[1024,256]{0,1:T(8,128)}) %all-reduce.11.cloned.1.call-update) | async-done | bytes 1048592 | tf_op jit(solution)/shard_map/psum | solution.py:12
  675.3 12.2 %fusion.1 = f32[1,2048,1,1024]{1,3,2,0:T(8,128)} fusion(f32[2048,1024]{0,1:T(8,128)} %copy-done, f32[2048,256]{0,1:T(8,128)S(1)} %copy-done.1, f32[1024,256]{0,1:T(8,128)} %all-reduce.11.cloned.1.call-done, pred[1024]{0:T(1024)(128)(4,1)S(1)} %fusion.37, pred[2048]{0:T(1024)(128)(4,1)S(1)} %fusion.29), kind=kOutput, calls=%fused_computation.4 | convolution fusion | flops 6448742400 | bytes 19926016 | tf_op jit(solution)/shard_map/dot_general | solution.py:60
  687.5 20.5 %copy.29 = f32[1,2048,1,1024]{3,2,1,0:T(1,128)} copy(f32[1,2048,1,1024]{1,3,2,0:T(8,128)} %fusion.1) | data formatting | bytes 16777216 | tf_op jit(solution)/shard_map/broadcast_in_dim | solution.py:65
  (50 shorter events, 13.8 us)
Async XLA Ops:
  6.5 114.2 %all-gather.2.cloned.1.call-start = ((), (), s32[]{:S(2)}) async-start(), calls=%async_computation.1 | async-start | bytes 33816576 | tf_op jit(solution)/shard_map/all_gather | solution.py:29
  163.7 117.1 %all-to-all-start = ((f32[128,4,16,256]{3,1,0,2:T(4,128)}), f32[128,4,16,256]{3,1,0,2:T(4,128)}, u32[]{:S(2)}, u32[]{:S(2)}) async-start(f32[128,4,16,256]{3,1,0,2:T(4,128)} %copy.20), calls=%async_computation | async-start | bytes 16777216 | tf_op jit(solution)/shard_map/all_to_all | solution.py:35
  168.4 217.3 %all-reduce.7.cloned.1.call-start = ((), (), s32[]{:S(2)}) async-start(), calls=%async_computation.2 | async-start | bytes 524288 | tf_op jit(solution)/shard_map/psum | solution.py:12
  289.7 9.2 %copy-start.2 = (f32[1,2048]{1,0:T(1,128)S(1)}, f32[1,2048]{1,0:T(1,128)}, u32[]{:S(2)}) copy-start(f32[1,2048]{1,0:T(1,128)} %param.3) | copy-start | bytes 24580
  302.9 3.4 copy-start
  307.1 272.3 %all-reduce.9.cloned.1.call-start = ((), (), s32[]{:S(2)}) async-start(), calls=%async_computation.3 | async-start | bytes 4194304 | tf_op jit(solution)/shard_map/psum | solution.py:12
  453.7 221.6 %all-reduce.11.cloned.1.call-start = ((), (), s32[]{:S(2)}) async-start(), calls=%async_computation.4 | async-start | bytes 2097152 | tf_op jit(solution)/shard_map/psum | solution.py:12
  579.4 95.9 %copy-start.1 = (f32[2048,256]{0,1:T(8,128)S(1)}, f32[2048,256]{0,1:T(8,128)}, u32[]{:S(2)}) copy-start(f32[2048,256]{0,1:T(8,128)} %all-reduce.9.cloned.1.call-done) | copy-start | bytes 6291460
Sparse Core Ops, SparseCore 0:
  10.4 110.3 all-gather.1
  307.2 78.5 all-reduce.6
  453.8 125.5 all-reduce.8
  590.1 85.2 all-reduce.10
where the time goes:
time: 723 us; the launch traced here: 715 us
  waiting for transfers between devices  506 us (70%)
  local copies, waits for them, and re-layouts  75.8 us (10%)
  other arithmetic  65.2 us (9%)
  matrix products  37.6 us (5%)
  between operations  14.9 us (2%)
  starting transfers between devices  14.8 us (2%)
    psum x3, waiting for transfers between devices, from_root(): return lax.psum(jnp.where(mine, array, jnp.zeros_like(array)), axis)  290 us
    all_gather x1, waiting for transfers between devices, local(): lax.all_gather(factors, ('prow', 'pcol'), axis=1, tiled=True)[0]  114 us
    all_to_all x1, waiting for transfers between devices, local(): lax.all_to_all(schur_rows, 'pcol', split_axis=2, concat_axis=0, tiled=True)  102 us
    another operation x6, other arithmetic, local(): diagonal_factor = jnp.linalg.cholesky(corner_tile)  34 us
    broadcast_in_dim x1, local copies, waits for them, and re-layouts, local(): return updated[None, :, None, :]  20.5 us
    another operation x3, other arithmetic, local(): lax.linalg.triangular_solve(diagonal_factor, column, left_side=False, low...  19.7 us
    dot_general x1, matrix products, local(): lax.dot_general(owned_rows, lax.all_gather(factors, ('prow', 'pcol'), axi...  19.3 us
  transfers between devices with their start and end apart: 5, of which 5 were waited for; matrix products, arithmetic and copies ran while one was open for 0% of the time, Pallas kernels for 0%

commit v1 on v0

v1 whole, which is shorter than its diff:
```python
import jax
import jax.numpy as jnp
from jax import lax
from jax.experimental import pallas as pl
from jax.experimental.pallas import tpu as pltpu
from jax.sharding import PartitionSpec as P

NB = 256
OB = 32
SHARD = 128
R = 1024
TILES = 8
NPCOL = 16
f32 = jnp.float32
bf16 = jnp.bfloat16
HIGHEST = lax.Precision.HIGHEST
NT = (((1,), (1,)), ((), ()))
NN = (((1,), (0,)), ((), ()))
TN = (((0,), (0,)), ((), ()))


def device_of(y, zh, zl, x, core):
    return ((y * 2 + zh) * NPCOL) + (zl * 4 + x) * 2 + core


def every():
    return [
        (y, zh, zl, x, core)
        for y in range(4) for zh in range(2) for zl in range(2) for x in range(4) for core in range(2)
    ]


def moves(step):
    return [(device_of(*at), device_of(*step(*at))) for at in every()]


def along_x(d):
    return moves(lambda y, zh, zl, x, core: (y, zh, zl, (x + d) % 4, core))


def along_y(d):
    return moves(lambda y, zh, zl, x, core: ((y + d) % 4, zh, zl, x, core))


def swap_zl():
    return moves(lambda y, zh, zl, x, core: (y, zh, 1 - zl, x, core))


def swap_zh():
    return moves(lambda y, zh, zl, x, core: (y, 1 - zh, zl, x, core))


def swap_core():
    return moves(lambda y, zh, zl, x, core: (y, zh, zl, x, 1 - core))


def to_columns():
    pairs = []
    for p in range(8):
        for j in range(NPCOL):
            c, b, h = j // 4, j // 2 % 2, j % 2
            pairs.append((p * NPCOL + j, (2 * c + h) * NPCOL + 8 * b + p))
    return pairs


def hop(at, axis, d):
    y, zh, zl, x, core = at
    if axis == "x":
        return (y, zh, zl, (x + d) % 4, core)
    if axis == "y":
        return ((y + d) % 4, zh, zl, x, core)
    z = (zh * 2 + zl + d) % 4
    return (y, z // 2, z % 2, x, core)


def spread_rounds():
    held = {0: [(0, 0, 0, 0, 0)], 1: [(0, 0, 0, 0, 1)]}
    order = {0: "xyz", 1: "yzx"}
    rounds = []
    for step in range(3):
        ops = []
        fresh = {0: [], 1: []}
        for d in (1, 3, 2):
            pairs = []
            for core in range(2):
                for at in held[core]:
                    to = hop(at, order[core][step], d)
                    pairs.append((device_of(*at), device_of(*to)))
                    fresh[core].append(to)
            ops.append(pairs)
        for core in range(2):
            held[core] = held[core] + fresh[core]
        rounds.append(ops)
    return rounds


def split(x):
    hi = x.astype(bf16)
    return hi, (x - hi.astype(f32)).astype(bf16)


def dot(a, b, dims):
    return lax.dot_general(a, b, dims, preferred_element_type=f32)


def factor_rows(a):
    for k0 in range(0, NB, OB):
        for k in range(k0, k0 + OB, 8):
            m = k0 + OB - k
            rows = a[pl.ds(k, m), :]
            cols = [jnp.broadcast_to(rows[:, k + j:k + j + 1], (m, 128)) for j in range(8)]
            sub = lax.broadcasted_iota(jnp.int32, (m, 128), 0)
            done = []
            for j in range(8):
                scale = lax.rsqrt(jnp.broadcast_to(cols[j][j:j + 1, :], (m, 128)))
                u = cols[j] * scale
                for l in range(j + 1, 8):
                    cols[l] = cols[l] - u * jnp.broadcast_to(u[l:l + 1, :], (m, 128))
                row = jnp.concatenate(
                    [rows[j:j + 1, 128 * c:128 * c + 128] * scale[0:1, :] for c in range(4)], 1
                )
                done.append(row)
                below = jnp.where(sub > j, u, 0.0)
                rows = rows - jnp.concatenate(
                    [below * jnp.broadcast_to(row[:, 128 * c:128 * c + 128], (m, 128)) for c in range(4)], 1
                )
            a[pl.ds(k, 8), :] = jnp.concatenate(done, 0)
            if m > 8:
                a[pl.ds(k + 8, m - 8), :] = rows[8:]
        if k0 + OB < NB:
            top = a[pl.ds(k0, OB), :]
            lo = (k0 + OB) // 128 * 128
            update = lax.dot_general(
                top[:, lo:NB], top, TN, preferred_element_type=f32, precision=HIGHEST
            )
            a[pl.ds(k0 + OB, NB - k0 - OB), :] -= update[k0 + OB - lo:]


def factor_kernel(core_ref, own_ref, other_ref, chol_ref, ghi_ref, glo_ref, lead, a):
    core = core_ref[0]
    lead[pl.ds(pl.multiple_of(core * SHARD, SHARD), SHARD), :] = own_ref[:SHARD, :]
    lead[pl.ds(pl.multiple_of((1 - core) * SHARD, SHARD), SHARD), :] = other_ref[:SHARD, :]
    coded = own_ref[SHARD:SHARD + 16, :].astype(f32)[0:1, :]
    shift = coded[:, :NB] + coded[:, NB:2 * NB] + coded[:, 2 * NB:3 * NB]
    row = lax.broadcasted_iota(jnp.int32, (NB, NB), 0)
    col = lax.broadcasted_iota(jnp.int32, (NB, NB), 1)
    f0 = lead[...]
    a[:, :NB] = dot(f0, f0, NT) + jnp.where(row == col, shift, 0.0)
    a[:, NB:] = jnp.where(row == col, 1.0, 0.0)
    factor_rows(a)
    chol_ref[...] = jnp.where(col >= row, a[:, :NB], 0.0)
    whi, wlo = split(a[:, NB:])
    g = dot(whi, f0, NN) + dot(wlo, f0, NN)
    ghi, glo = split(g)
    ghi_ref[...] = ghi
    glo_ref[...] = glo


def factor(core, own, other):
    vm = pl.BlockSpec(memory_space=pltpu.VMEM)
    return pl.pallas_call(
        factor_kernel,
        out_shape=[
            jax.ShapeDtypeStruct((NB, NB), f32),
            jax.ShapeDtypeStruct((NB, R), bf16),
            jax.ShapeDtypeStruct((NB, R), bf16),
        ],
        in_specs=[pl.BlockSpec(memory_space=pltpu.SMEM), vm, vm],
        out_specs=[vm, vm, vm],
        scratch_shapes=[pltpu.VMEM((NB, R), bf16), pltpu.VMEM((NB, 2 * NB), f32)],
        compiler_params=pltpu.CompilerParams(vmem_limit_bytes=32 << 20),
    )(core, own, other)


def tail_kernel(at_ref, *refs):
    fs = refs[0:8]
    cs = refs[8:12]
    shift_ref, chol_ref, ghi_ref, glo_ref, out_ref, f, a, hhi, hlo, sem = refs[12:]
    p, q = at_ref[0], at_ref[1]
    y, zh = p // 2, p % 2
    zl, x, core = q // 8, q // 2 % 4, q % 2
    g = pl.program_id(0)

    def copies():
        out = []
        for n, d in enumerate((0, 1, 3, 2)):
            for dz in range(2):
                for own in range(2):
                    tile = (zl + dz) % 2 * 4 + (x - d + 4) % 4
                    shard = tile * 2 + (core + own) % 2
                    out.append(pltpu.make_async_copy(
                        fs[n * 2 + own].at[dz],
                        f.at[pl.ds(pl.multiple_of(shard * SHARD, SHARD), SHARD), :],
                        sem.at[0],
                    ))
                row = (y - d + 4) % 4 * 2 + (zh + dz) % 2
                out.append(pltpu.make_async_copy(
                    cs[n].at[dz],
                    a.at[pl.ds(pl.multiple_of(row * SHARD, SHARD), SHARD), :],
                    sem.at[0],
                ))
        return out

    @pl.when(g == 0)
    def _():
        for copy in copies():
            copy.start()
        for copy in copies():
            copy.wait()
        for c in range(4):
            at = pl.ds(c * NB, NB)
            ac = a[at, :]
            lhi, llo = split(dot(ac, ghi_ref[...], NT) + dot(ac, glo_ref[...], NT))
            h = ac.astype(f32) - (
                dot(lhi, ghi_ref[...], NN) + dot(lhi, glo_ref[...], NN) + dot(llo, ghi_ref[...], NN)
            )
            hi, lo = split(h)
            hhi[at, :] = hi
            hlo[at, :] = lo

        @pl.when(q == 0)
        def _():
            hhi[pl.ds(0, NB), :] = ghi_ref[...]
            hlo[pl.ds(0, NB), :] = glo_ref[...]

    ft = f[pl.ds(pl.multiple_of(g * NB, NB), NB), :]
    leading = (g == 0) & (p == 0)
    row = lax.broadcasted_iota(jnp.int32, (NB, NB), 0)
    col = lax.broadcasted_iota(jnp.int32, (NB, NB), 1)
    shift = shift_ref[pl.ds(g, 1), :]
    for c in range(4):
        at = pl.ds(c * NB, NB)
        ours = (p == q % 8) & (g == 2 * c + q // 8)
        diagonal = jnp.where((row == col) & ours, shift, 0.0)

        def put(value):
            for n in range(2):
                out_ref[:, 2 * c + n, :] = value[:, n * 128:n * 128 + 128]

        @pl.when(leading)
        def _():
            put(dot(ft, a[at, :], NT) + diagonal)

        @pl.when(jnp.logical_not(leading))
        def _():
            put(dot(ft, hhi[at, :], NT) + dot(ft, hlo[at, :], NT) + diagonal)

    @pl.when(leading & (q == 0))
    def _():
        lower = chol_ref[...].T
        for n in range(2):
            out_ref[:, n, :] = lower[:, n * 128:n * 128 + 128]


def tail(at, fs, cs, shift, chol, ghi, glo):
    hbm = pl.BlockSpec(memory_space=pl.ANY)
    vm = pl.BlockSpec(memory_space=pltpu.VMEM)
    return pl.pallas_call(
        tail_kernel,
        grid=(TILES,),
        out_shape=jax.ShapeDtypeStruct((TILES * NB, 8, 128), f32),
        in_specs=[pl.BlockSpec(memory_space=pltpu.SMEM)] + [hbm] * 12 + [vm] * 4,
        out_specs=pl.BlockSpec((NB, 8, 128), lambda g: (g, 0, 0)),
        scratch_shapes=[
            pltpu.VMEM((TILES * NB, R), bf16),
            pltpu.VMEM((4 * NB, R), bf16),
            pltpu.VMEM((4 * NB, R), bf16),
            pltpu.VMEM((4 * NB, R), bf16),
            pltpu.SemaphoreType.DMA((1,)),
        ],
        compiler_params=pltpu.CompilerParams(vmem_limit_bytes=40 << 20),
    )(at, *fs, *cs, shift, chol, ghi, glo)


def local(factors, shift):
    both = ("prow", "pcol")
    p = lax.axis_index("prow")
    q = lax.axis_index("pcol")
    own = factors[0]

    def send(value, pairs):
        return lax.ppermute(value, both, pairs)

    s = shift[:, :NB]
    s0 = lax.reduce_precision(s, 8, 7)
    s1 = lax.reduce_precision(s - s0, 8, 7)
    s2 = s - s0 - s1
    coded = jnp.concatenate([s0, s1, s2, jnp.zeros_like(s)], 1).astype(bf16)
    lead = jnp.concatenate([own, coded, jnp.zeros((15, R), bf16)], 0)
    lead = jnp.where((p == 0) & (q < 2), lead, jnp.zeros_like(lead))
    for ops in spread_rounds():
        got = [send(lead, pairs) for pairs in ops]
        lead = lead + (got[0] + got[1] + got[2])
    lead_other = send(lead, swap_core())
    chol, ghi, glo = factor(q[None] % 2, lead, lead_other)

    pair = jnp.stack([own, send(own, swap_zl())])
    rows = [pair] + [send(pair, along_x(d)) for d in (1, 3, 2)]
    fs = []
    for value in rows:
        fs += [value, send(value, swap_core())]

    piece = send(own, to_columns())
    piece = jnp.stack([piece, send(piece, swap_zh())])
    cs = [piece] + [send(piece, along_y(d)) for d in (1, 3, 2)]

    out = tail(jnp.stack([p, q]), fs, cs, shift.reshape(TILES, NB), chol, ghi, glo)
    return out.reshape(1, TILES * NB, 1, 4 * NB)


def solution(mesh):
    in_specs = (P("prow", "pcol", None), P("prow", None))
    out_specs = P("prow", None, "pcol", None)
    return jax.shard_map(local, mesh=mesh, in_specs=in_specs, out_specs=out_specs, check_vma=False)
```

time: 723 us -> 113 us (0.16)
  the two profiles are of different devices: /device:TPU:1 before, /device:TPU:31 now
where the time goes in v1:
time: 113 us; the launch traced here: 112 us
  Pallas kernels  37.5 us (33%)
  waiting for transfers between devices  35.6 us (32%)
  starting transfers between devices  28.8 us (25%)
  other arithmetic  5.51 us (5%)
  local copies, waits for them, and re-layouts  4.19 us (4%)
    ppermute x23, waiting for transfers between devices, send(): return lax.ppermute(value, both, pairs)  35.6 us
    ppermute x23, starting transfers between devices, send(): return lax.ppermute(value, both, pairs)  28.8 us
    pallas_call x1, Pallas kernels, tail(): pl.pallas_call(tail_kernel, grid=(TILES,), out_shape=jax.ShapeDtypeStruct...  27.1 us
    pallas_call x1, Pallas kernels, factor(): pl.pallas_call(factor_kernel, out_shape=[jax.ShapeDtypeStruct((NB, NB), f...  10.3 us
    unnamed x9, local copies, waits for them, and re-layouts  4.1 us
  transfers between devices with their start and end apart: 23, of which 4 were waited for; matrix products, arithmetic and copies ran while one was open for 3% of the time, Pallas kernels for 9%

profile of v1, /device:TPU:31, one launch (start us, length us, event | category | flops | bytes accessed | tf_op | source)
XLA Modules:
  0.0 111.9 jit_solution(17050284085695524463)
XLA Ops:
  0.0 0.7 reduce-precision_convert_fusion.1
  0.8 1.1 maximum_select_fusion
  4.0 1.2 %add_add_fusion.2 = bf16[144,1024]{1,0:T(8,128)(2,1)S(1)} fusion(bf16[144,1024]{1,0:T(8,128)(2,1)S(1)} %collective-permute-done.15, bf16[144,1024]{1,0:T(8,128)(2,1)S(1)} %collective-permute-done.13, bf16[144,1024]{1,0:T(8,128)(2,1)S(1)} %collective-permute-done.14, bf16[144]{0:T(256)(128)(2,1)S(1)} %pad.5.clone, bf16[1,256]{1,0:T(2,128)(2,1)S(1)} %broadcast_in_dim.10, ...), kind=kLoop, calls=%fused_computation.5 | loop fusion | flops 3096576 | bytes 1444129 | tf_op jit(solution)/shard_map/add | solution.py:293
  7.2 6.9 %collective-permute-start.8 = (bf16[128,1024]{1,0:T(8,128)(2,1)}, bf16[128,1024]{1,0:T(8,128)(2,1)S(1)}, u32[]{:S(2)}, u32[]{:S(2)}) collective-permute-start(bf16[128,1024]{1,0:T(8,128)(2,1)} %bitcast.9), channel_id=1, source_target_pairs={{0,0},{1,16},{2,8},{3,24},{4,32},{5,48},{6,40},{7,56},{8,64},{9,80... | collective-permute-start | bytes 786440 | tf_op jit(solution)/shard_map/ppermute | solution.py:282
  14.2 10.4 %collective-permute-done.8 = bf16[128,1024]{1,0:T(8,128)(2,1)S(1)} collective-permute-done((bf16[128,1024]{1,0:T(8,128)(2,1)}, bf16[128,1024]{1,0:T(8,128)(2,1)S(1)}, u32[]{:S(2)}, u32[]{:S(2)}) %collective-permute-start.8) | collective-permute-done | bytes 262176 | tf_op jit(solution)/shard_map/ppermute | solution.py:282
  24.6 1.2 %collective-permute-start.9 = (bf16[128,1024]{1,0:T(8,128)(2,1)S(1)}, bf16[128,1024]{1,0:T(8,128)(2,1)S(1)}, u32[]{:S(2)}, u32[]{:S(2)}) collective-permute-start(bf16[128,1024]{1,0:T(8,128)(2,1)S(1)} %collective-permute-done.8), channel_id=1, source_target_pairs={{0,16},{1,17},{2,18},{3,19},{4,20},{5,21},{6,22},{7,23},{8,24},{9,... | collective-permute-start | bytes 786440 | tf_op jit(solution)/shard_map/ppermute | solution.py:282
  26.6 1.3 %collective-permute-start.20 = (bf16[144,1024]{1,0:T(8,128)(2,1)S(1)}, bf16[144,1024]{1,0:T(8,128)(2,1)S(1)}, u32[]{:S(2)}, u32[]{:S(2)}) collective-permute-start(bf16[144,1024]{1,0:T(8,128)(2,1)S(1)} %add_add_fusion.1), channel_id=1, source_target_pairs={{0,24},{2,26},{6,30},{4,28},{32,56},{34,58},{38,62},{36,60},{96,12... | collective-permute-start | bytes 884744 | tf_op jit(solution)/shard_map/ppermute | solution.py:282
  28.6 1.0 pad_maximum_fusion.refs_0_
  29.6 4.9 %collective-permute-start.6 = (bf16[2,128,1024]{2,1,0:T(8,128)(2,1)S(1)}, bf16[2,128,1024]{2,1,0:T(8,128)(2,1)S(1)}, u32[]{:S(2)}, u32[]{:S(2)}) collective-permute-start(bf16[2,128,1024]{2,1,0:T(8,128)(2,1)S(1)} %pad_maximum_fusion.refs_0_), channel_id=1, source_target_pairs={{0,4},{1,5},{2,6},{3,7},{4,0},{5,1},{6,2},{7,3},{8,12},{9,13},{10,... | collective-permute-start | bytes 1572872 | tf_op jit(solution)/shard_map/ppermute | solution.py:282
  34.5 2.5 %collective-permute-start.4 = (bf16[2,128,1024]{2,1,0:T(8,128)(2,1)S(1)}, bf16[2,128,1024]{2,1,0:T(8,128)(2,1)S(1)}, u32[]{:S(2)}, u32[]{:S(2)}) collective-permute-start(bf16[2,128,1024]{2,1,0:T(8,128)(2,1)S(1)} %pad_maximum_fusion.refs_0_), channel_id=1, source_target_pairs={{0,6},{1,7},{2,0},{3,1},{4,2},{5,3},{6,4},{7,5},{8,14},{9,15},{10,... | collective-permute-start | bytes 1572872 | tf_op jit(solution)/shard_map/ppermute | solution.py:282
  37.0 0.9 collective-permute-start.2
  37.9 14.0 %collective-permute-done.20 = bf16[144,1024]{1,0:T(8,128)(2,1)S(1)} collective-permute-done((bf16[144,1024]{1,0:T(8,128)(2,1)S(1)}, bf16[144,1024]{1,0:T(8,128)(2,1)S(1)}, u32[]{:S(2)}, u32[]{:S(2)}) %collective-permute-start.20) | collective-permute-done | bytes 294944 | tf_op jit(solution)/shard_map/ppermute | solution.py:282
  52.5 8.3 %collective-permute-done.4.refs_4_ = bf16[2,128,1024]{2,1,0:T(8,128)(2,1)S(1)} collective-permute-done((bf16[2,128,1024]{2,1,0:T(8,128)(2,1)S(1)}, bf16[2,128,1024]{2,1,0:T(8,128)(2,1)S(1)}, u32[]{:S(2)}, u32[]{:S(2)}) %collective-permute-start.4) | collective-permute-done | bytes 524320 | tf_op jit(solution)/shard_map/ppermute | solution.py:282
  60.8 0.9 collective-permute-start.11
  61.7 1.8 %collective-permute-start.10 = (bf16[2,128,1024]{2,1,0:T(8,128)(2,1)S(1)}, bf16[2,128,1024]{2,1,0:T(8,128)(2,1)}, u32[]{:S(2)}, u32[]{:S(2)}) collective-permute-start(bf16[2,128,1024]{2,1,0:T(8,128)(2,1)S(1)} %pad_maximum_fusion.1.refs_8_), channel_id=1, source_target_pairs={{0,32},{1,33},{2,34},{3,35},{4,36},{5,37},{6,38},{7,39},{8,40},{9,... | collective-permute-start | bytes 1572872 | tf_op jit(solution)/shard_map/ppermute | solution.py:282
  63.5 2.9 %collective-permute-done.12.refs_11_ = bf16[2,128,1024]{2,1,0:T(8,128)(2,1)S(1)} collective-permute-done((bf16[2,128,1024]{2,1,0:T(8,128)(2,1)S(1)}, bf16[2,128,1024]{2,1,0:T(8,128)(2,1)S(1)}, u32[]{:S(2)}, u32[]{:S(2)}) %collective-permute-start.12) | collective-permute-done | bytes 524320 | tf_op jit(solution)/shard_map/ppermute | solution.py:282
  66.4 0.8 copy-done
  67.2 2.3 %collective-permute-start.5 = (bf16[2,128,1024]{2,1,0:T(8,128)(2,1)S(1)}, bf16[2,128,1024]{2,1,0:T(8,128)(2,1)}, u32[]{:S(2)}, u32[]{:S(2)}) collective-permute-start(bf16[2,128,1024]{2,1,0:T(8,128)(2,1)S(1)} %collective-permute-done.4.refs_4_), channel_id=1, source_target_pairs={{0,1},{1,0},{2,3},{3,2},{4,5},{5,4},{6,7},{7,6},{8,9},{9,8},{10,11... | collective-permute-start | bytes 1572872 | tf_op jit(solution)/shard_map/ppermute | solution.py:282
  69.5 0.7 copy-done.2
  70.8 1.3 %reduce.3 = f32[2048]{0:T(1024)S(1)} reduce(f32[1,2048]{1,0:T(1,128)} %param.3, f32[]{:T(128)} %broadcast.19), dimensions={0}, to_apply=%param.3.reduce_sub_computation.3 | reduce | bytes 16388 | tf_op args[1]
  72.3 1.0 copy-done.3
  73.2 10.3 %shard_map.28 = (f32[256,256]{1,0:T(8,128)S(1)}, bf16[256,1024]{1,0:T(8,128)(2,1)S(1)}, bf16[256,1024]{1,0:T(8,128)(2,1)S(1)}) custom-call(s32[1]{0:T(128)S(6)} %select_n.15.core_ref, bf16[144,1024]{1,0:T(8,128)(2,1)S(1)} %add_add_fusion.own_ref, bf16[144,1024]{1,0:T(8,128)(2,1)S(1)} %copy-done.3), custom_call_target="tpu_custom_call" | custom-call | tf_op jit(solution)/shard_map/pallas_call | solution.py:161
  83.6 1.0 copy-done.1
  84.7 27.1 %shard_map.29 = f32[2048,8,128]{2,1,0:T(8,128)} custom-call(s32[2]{0:T(128)S(1)} %pad_add_fusion.at_ref, bf16[2,128,1024]{2,1,0:T(8,128)(2,1)S(1)} %pad_maximum_fusion.refs_0_, bf16[2,128,1024]{2,1,0:T(8,128)(2,1)S(1)} %collective-permute-done.1.refs_1_, bf16[2,128,1024]{2,1,0:T(8,128)(2,1)S(1)} %collective-permute-done.2.refs_2_, ...), custom_call_target="tpu_custom_call" | custom-call | tf_op jit(solution)/shard_map/pallas_call | solution.py:258
  (46 shorter events, 7.1 us)
Async XLA Ops:
  1.9 2.1 %collective-permute-start.15 = (bf16[144,1024]{1,0:T(8,128)(2,1)S(1)}, bf16[144,1024]{1,0:T(8,128)(2,1)S(1)}, u32[]{:S(2)}, u32[]{:S(2)}) collective-permute-start(bf16[144,1024]{1,0:T(8,128)(2,1)S(1)} %maximum_select_fusion), channel_id=1, source_target_pairs={{0,4},{1,65}} | collective-permute-start | bytes 884744 | tf_op jit(solution)/shard_map/ppermute | solution.py:282
  2.5 1.4 %collective-permute-start.14 = (bf16[144,1024]{1,0:T(8,128)(2,1)S(1)}, bf16[144,1024]{1,0:T(8,128)(2,1)S(1)}, u32[]{:S(2)}, u32[]{:S(2)}) collective-permute-start(bf16[144,1024]{1,0:T(8,128)(2,1)S(1)} %maximum_select_fusion), channel_id=1, source_target_pairs={{0,6},{1,97}} | collective-permute-start | bytes 884744 | tf_op jit(solution)/shard_map/ppermute | solution.py:282
  3.2 0.7 collective-permute-start.13
  5.1 20.7 %collective-permute-start.18 = (bf16[144,1024]{1,0:T(8,128)(2,1)S(1)}, bf16[144,1024]{1,0:T(8,128)(2,1)S(1)}, u32[]{:S(2)}, u32[]{:S(2)}) collective-permute-start(bf16[144,1024]{1,0:T(8,128)(2,1)S(1)} %add_add_fusion.2), channel_id=1, source_target_pairs={{0,64},{2,66},{6,70},{4,68},{1,17},{33,49},{97,113},{65,81}} | collective-permute-start | bytes 884744 | tf_op jit(solution)/shard_map/ppermute | solution.py:282
  5.8 20.0 %collective-permute-start.17 = (bf16[144,1024]{1,0:T(8,128)(2,1)S(1)}, bf16[144,1024]{1,0:T(8,128)(2,1)S(1)}, u32[]{:S(2)}, u32[]{:S(2)}) collective-permute-start(bf16[144,1024]{1,0:T(8,128)(2,1)S(1)} %add_add_fusion.2), channel_id=1, source_target_pairs={{0,96},{2,98},{6,102},{4,100},{1,25},{33,57},{97,121},{65,89}} | collective-permute-start | bytes 884744 | tf_op jit(solution)/shard_map/ppermute | solution.py:282
  6.5 19.3 %collective-permute-start.16 = (bf16[144,1024]{1,0:T(8,128)(2,1)S(1)}, bf16[144,1024]{1,0:T(8,128)(2,1)S(1)}, u32[]{:S(2)}, u32[]{:S(2)}) collective-permute-start(bf16[144,1024]{1,0:T(8,128)(2,1)S(1)} %add_add_fusion.2), channel_id=1, source_target_pairs={{0,32},{2,34},{6,38},{4,36},{1,9},{33,41},{97,105},{65,73}} | collective-permute-start | bytes 884744 | tf_op jit(solution)/shard_map/ppermute | solution.py:282
  7.2 17.4 %collective-permute-start.8 = (bf16[128,1024]{1,0:T(8,128)(2,1)}, bf16[128,1024]{1,0:T(8,128)(2,1)S(1)}, u32[]{:S(2)}, u32[]{:S(2)}) collective-permute-start(bf16[128,1024]{1,0:T(8,128)(2,1)} %bitcast.9), channel_id=1, source_target_pairs={{0,0},{1,16},{2,8},{3,24},{4,32},{5,48},{6,40},{7,56},{8,64},{9,80... | collective-permute-start | bytes 786440 | tf_op jit(solution)/shard_map/ppermute | solution.py:282
  14.1 14.5 %collective-permute-start = (bf16[128,1024]{1,0:T(8,128)(2,1)}, bf16[128,1024]{1,0:T(8,128)(2,1)S(1)}, u32[]{:S(2)}, u32[]{:S(2)}) collective-permute-start(bf16[128,1024]{1,0:T(8,128)(2,1)} %bitcast.10), channel_id=1, source_target_pairs={{0,8},{1,9},{2,10},{3,11},{4,12},{5,13},{6,14},{7,15},{8,0},{9,1},... | collective-permute-start | bytes 786440 | tf_op jit(solution)/shard_map/ppermute | solution.py:282
  24.6 9.9 %collective-permute-start.9 = (bf16[128,1024]{1,0:T(8,128)(2,1)S(1)}, bf16[128,1024]{1,0:T(8,128)(2,1)S(1)}, u32[]{:S(2)}, u32[]{:S(2)}) collective-permute-start(bf16[128,1024]{1,0:T(8,128)(2,1)S(1)} %collective-permute-done.8), channel_id=1, source_target_pairs={{0,16},{1,17},{2,18},{3,19},{4,20},{5,21},{6,22},{7,23},{8,24},{9,... | collective-permute-start | bytes 786440 | tf_op jit(solution)/shard_map/ppermute | solution.py:282
  25.9 11.1 %collective-permute-start.21 = (bf16[144,1024]{1,0:T(8,128)(2,1)S(1)}, bf16[144,1024]{1,0:T(8,128)(2,1)S(1)}, u32[]{:S(2)}, u32[]{:S(2)}) collective-permute-start(bf16[144,1024]{1,0:T(8,128)(2,1)S(1)} %add_add_fusion.1), channel_id=1, source_target_pairs={{0,16},{2,18},{6,22},{4,20},{32,48},{34,50},{38,54},{36,52},{96,11... | collective-permute-start | bytes 884744 | tf_op jit(solution)/shard_map/ppermute | solution.py:282
  26.6 25.3 %collective-permute-start.20 = (bf16[144,1024]{1,0:T(8,128)(2,1)S(1)}, bf16[144,1024]{1,0:T(8,128)(2,1)S(1)}, u32[]{:S(2)}, u32[]{:S(2)}) collective-permute-start(bf16[144,1024]{1,0:T(8,128)(2,1)S(1)} %add_add_fusion.1), channel_id=1, source_target_pairs={{0,24},{2,26},{6,30},{4,28},{32,56},{34,58},{38,62},{36,60},{96,12... | collective-permute-start | bytes 884744 | tf_op jit(solution)/shard_map/ppermute | solution.py:282
  27.9 24.0 %collective-permute-start.19 = (bf16[144,1024]{1,0:T(8,128)(2,1)S(1)}, bf16[144,1024]{1,0:T(8,128)(2,1)S(1)}, u32[]{:S(2)}, u32[]{:S(2)}) collective-permute-start(bf16[144,1024]{1,0:T(8,128)(2,1)S(1)} %add_add_fusion.1), channel_id=1, source_target_pairs={{0,8},{2,10},{6,14},{4,12},{32,40},{34,42},{38,46},{36,44},{96,104... | collective-permute-start | bytes 884744 | tf_op jit(solution)/shard_map/ppermute | solution.py:282
  29.6 22.4 %collective-permute-start.6 = (bf16[2,128,1024]{2,1,0:T(8,128)(2,1)S(1)}, bf16[2,128,1024]{2,1,0:T(8,128)(2,1)S(1)}, u32[]{:S(2)}, u32[]{:S(2)}) collective-permute-start(bf16[2,128,1024]{2,1,0:T(8,128)(2,1)S(1)} %pad_maximum_fusion.refs_0_), channel_id=1, source_target_pairs={{0,4},{1,5},{2,6},{3,7},{4,0},{5,1},{6,2},{7,3},{8,12},{9,13},{10,... | collective-permute-start | bytes 1572872 | tf_op jit(solution)/shard_map/ppermute | solution.py:282
  34.5 26.3 %collective-permute-start.4 = (bf16[2,128,1024]{2,1,0:T(8,128)(2,1)S(1)}, bf16[2,128,1024]{2,1,0:T(8,128)(2,1)S(1)}, u32[]{:S(2)}, u32[]{:S(2)}) collective-permute-start(bf16[2,128,1024]{2,1,0:T(8,128)(2,1)S(1)} %pad_maximum_fusion.refs_0_), channel_id=1, source_target_pairs={{0,6},{1,7},{2,0},{3,1},{4,2},{5,3},{6,4},{7,5},{8,14},{9,15},{10,... | collective-permute-start | bytes 1572872 | tf_op jit(solution)/shard_map/ppermute | solution.py:282
  37.0 24.7 %collective-permute-start.2 = (bf16[2,128,1024]{2,1,0:T(8,128)(2,1)S(1)}, bf16[2,128,1024]{2,1,0:T(8,128)(2,1)S(1)}, u32[]{:S(2)}, u32[]{:S(2)}) collective-permute-start(bf16[2,128,1024]{2,1,0:T(8,128)(2,1)S(1)} %pad_maximum_fusion.refs_0_), channel_id=1, source_target_pairs={{0,2},{1,3},{2,4},{3,5},{4,6},{5,7},{6,0},{7,1},{8,10},{9,11},{10,... | collective-permute-start | bytes 1572872 | tf_op jit(solution)/shard_map/ppermute | solution.py:282
  51.9 11.6 %collective-permute-start.1 = (bf16[2,128,1024]{2,1,0:T(8,128)(2,1)S(1)}, bf16[2,128,1024]{2,1,0:T(8,128)(2,1)S(1)}, u32[]{:S(2)}, u32[]{:S(2)}) collective-permute-start(bf16[2,128,1024]{2,1,0:T(8,128)(2,1)S(1)} %pad_maximum_fusion.refs_0_), channel_id=1, source_target_pairs={{0,1},{1,0},{2,3},{3,2},{4,5},{5,4},{6,7},{7,6},{8,9},{9,8},{10,11... | collective-permute-start | bytes 1572872 | tf_op jit(solution)/shard_map/ppermute | solution.py:282
  51.9 14.5 %collective-permute-start.12 = (bf16[2,128,1024]{2,1,0:T(8,128)(2,1)S(1)}, bf16[2,128,1024]{2,1,0:T(8,128)(2,1)S(1)}, u32[]{:S(2)}, u32[]{:S(2)}) collective-permute-start(bf16[2,128,1024]{2,1,0:T(8,128)(2,1)S(1)} %pad_maximum_fusion.1.refs_8_), channel_id=1, source_target_pairs={{0,64},{1,65},{2,66},{3,67},{4,68},{5,69},{6,70},{7,71},{8,72},{9,... | collective-permute-start | bytes 1572872 | tf_op jit(solution)/shard_map/ppermute | solution.py:282
  52.0 17.6 %collective-permute-start.22 = (bf16[144,1024]{1,0:T(8,128)(2,1)S(1)}, bf16[144,1024]{1,0:T(8,128)(2,1)S(1)}, u32[]{:S(2)}, u32[]{:S(2)}) collective-permute-start(bf16[144,1024]{1,0:T(8,128)(2,1)S(1)} %add_add_fusion.own_ref), channel_id=1, source_target_pairs={{0,1},{1,0},{2,3},{3,2},{4,5},{5,4},{6,7},{7,6},{8,9},{9,8},{10,11... | collective-permute-start | bytes 884744 | tf_op jit(solution)/shard_map/ppermute | solution.py:282
  60.8 22.8 %collective-permute-start.11 = (bf16[2,128,1024]{2,1,0:T(8,128)(2,1)S(1)}, bf16[2,128,1024]{2,1,0:T(8,128)(2,1)}, u32[]{:S(2)}, u32[]{:S(2)}) collective-permute-start(bf16[2,128,1024]{2,1,0:T(8,128)(2,1)S(1)} %pad_maximum_fusion.1.refs_8_), channel_id=1, source_target_pairs={{0,96},{1,97},{2,98},{3,99},{4,100},{5,101},{6,102},{7,103},{8,104... | collective-permute-start | bytes 1572872 | tf_op jit(solution)/shard_map/ppermute | solution.py:282
  61.7 21.9 %collective-permute-start.10 = (bf16[2,128,1024]{2,1,0:T(8,128)(2,1)S(1)}, bf16[2,128,1024]{2,1,0:T(8,128)(2,1)}, u32[]{:S(2)}, u32[]{:S(2)}) collective-permute-start(bf16[2,128,1024]{2,1,0:T(8,128)(2,1)S(1)} %pad_maximum_fusion.1.refs_8_), channel_id=1, source_target_pairs={{0,32},{1,33},{2,34},{3,35},{4,36},{5,37},{6,38},{7,39},{8,40},{9,... | collective-permute-start | bytes 1572872 | tf_op jit(solution)/shard_map/ppermute | solution.py:282
  63.5 20.1 %collective-permute-start.7 = (bf16[2,128,1024]{2,1,0:T(8,128)(2,1)S(1)}, bf16[2,128,1024]{2,1,0:T(8,128)(2,1)}, u32[]{:S(2)}, u32[]{:S(2)}) collective-permute-start(bf16[2,128,1024]{2,1,0:T(8,128)(2,1)S(1)} %collective-permute-done.6.refs_6_), channel_id=1, source_target_pairs={{0,1},{1,0},{2,3},{3,2},{4,5},{5,4},{6,7},{7,6},{8,9},{9,8},{10,11... | collective-permute-start | bytes 1572872 | tf_op jit(solution)/shard_map/ppermute | solution.py:282
  67.2 16.4 %collective-permute-start.5 = (bf16[2,128,1024]{2,1,0:T(8,128)(2,1)S(1)}, bf16[2,128,1024]{2,1,0:T(8,128)(2,1)}, u32[]{:S(2)}, u32[]{:S(2)}) collective-permute-start(bf16[2,128,1024]{2,1,0:T(8,128)(2,1)S(1)} %collective-permute-done.4.refs_4_), channel_id=1, source_target_pairs={{0,1},{1,0},{2,3},{3,2},{4,5},{5,4},{6,7},{7,6},{8,9},{9,8},{10,11... | collective-permute-start | bytes 1572872 | tf_op jit(solution)/shard_map/ppermute | solution.py:282
  70.3 13.3 %collective-permute-start.3 = (bf16[2,128,1024]{2,1,0:T(8,128)(2,1)S(1)}, bf16[2,128,1024]{2,1,0:T(8,128)(2,1)}, u32[]{:S(2)}, u32[]{:S(2)}) collective-permute-start(bf16[2,128,1024]{2,1,0:T(8,128)(2,1)S(1)} %collective-permute-done.2.refs_2_), channel_id=1, source_target_pairs={{0,1},{1,0},{2,3},{3,2},{4,5},{5,4},{6,7},{7,6},{8,9},{9,8},{10,11... | collective-permute-start | bytes 1572872 | tf_op jit(solution)/shard_map/ppermute | solution.py:282
  83.6 1.0 copy-start.1
  (3 other events, 2.5 us)

commit v2 on v1

v2 whole, which is shorter than its diff:
```python
import jax
import jax.numpy as jnp
from jax import lax
from jax.experimental import pallas as pl
from jax.experimental.pallas import tpu as pltpu
from jax.sharding import PartitionSpec as P

NB = 256
OB = 32
SHARD = 128
R = 1024
TILES = 8
NPCOL = 16
MB = 512
MSG = R + 384
STEPS = TILES * NB // MB
f32 = jnp.float32
bf16 = jnp.bfloat16
HIGHEST = lax.Precision.HIGHEST
NT = (((1,), (1,)), ((), ()))
NN = (((1,), (0,)), ((), ()))
TN = (((0,), (0,)), ((), ()))


def device_of(y, zh, zl, x, core):
    return ((y * 2 + zh) * NPCOL) + (zl * 4 + x) * 2 + core


def every():
    return [
        (y, zh, zl, x, core)
        for y in range(4) for zh in range(2) for zl in range(2) for x in range(4) for core in range(2)
    ]


def moves(step):
    return [(device_of(*at), device_of(*step(*at))) for at in every()]


def moves(step):
    return [(device_of(*at), device_of(*step(at))) for at in every()]


def swap_zl(at):
    y, zh, zl, x, core = at
    return (y, zh, 1 - zl, x, core)


def swap_zh(at):
    y, zh, zl, x, core = at
    return (y, 1 - zh, zl, x, core)


def swap_core(at):
    y, zh, zl, x, core = at
    return (y, zh, zl, x, 1 - core)


def to_columns():
    pairs = []
    for p in range(8):
        for j in range(NPCOL):
            c, b, h = j // 4, j // 2 % 2, j % 2
            pairs.append((p * NPCOL + j, (2 * c + h) * NPCOL + 8 * b + p))
    return pairs


def hop(at, axis, d):
    y, zh, zl, x, core = at
    if axis == "x":
        return (y, zh, zl, (x + d) % 4, core)
    if axis == "y":
        return ((y + d) % 4, zh, zl, x, core)
    z = (zh * 2 + zl + d) % 4
    return (y, z // 2, z % 2, x, core)


def spread_rounds():
    held = {0: [(0, 0, 0, 0, 0)], 1: [(0, 0, 0, 0, 1)]}
    order = {0: "xyz", 1: "yzx"}
    rounds = []
    for step in range(3):
        ops = []
        fresh = {0: [], 1: []}
        for d in (1, 3, 2):
            pairs = []
            for core in range(2):
                for at in held[core]:
                    to = hop(at, order[core][step], d)
                    pairs.append((device_of(*at), device_of(*to)))
                    fresh[core].append(to)
            ops.append(pairs)
        for core in range(2):
            held[core] = held[core] + fresh[core]
        rounds.append(ops)
    return rounds


def split(x):
    hi = x.astype(bf16)
    return hi, (x - hi.astype(f32)).astype(bf16)


def dot(a, b, dims):
    return lax.dot_general(a, b, dims, preferred_element_type=f32)


def factor_rows(a):
    for k0 in range(0, NB, OB):
        for k in range(k0, k0 + OB, 8):
            m = k0 + OB - k
            rows = a[pl.ds(k, m), :]
            cols = [jnp.broadcast_to(rows[:, k + j:k + j + 1], (m, 128)) for j in range(8)]
            sub = lax.broadcasted_iota(jnp.int32, (m, 128), 0)
            done = []
            for j in range(8):
                scale = lax.rsqrt(jnp.broadcast_to(cols[j][j:j + 1, :], (m, 128)))
                u = cols[j] * scale
                for l in range(j + 1, 8):
                    cols[l] = cols[l] - u * jnp.broadcast_to(u[l:l + 1, :], (m, 128))
                row = jnp.concatenate(
                    [rows[j:j + 1, 128 * c:128 * c + 128] * scale[0:1, :] for c in range(4)], 1
                )
                done.append(row)
                below = jnp.where(sub > j, u, 0.0)
                rows = rows - jnp.concatenate(
                    [below * jnp.broadcast_to(row[:, 128 * c:128 * c + 128], (m, 128)) for c in range(4)], 1
                )
            a[pl.ds(k, 8), :] = jnp.concatenate(done, 0)
            if m > 8:
                a[pl.ds(k + 8, m - 8), :] = rows[8:]
        if k0 + OB < NB:
            top = a[pl.ds(k0, OB), :]
            lo = (k0 + OB) // 128 * 128
            update = lax.dot_general(
                top[:, lo:NB], top, TN, preferred_element_type=f32, precision=HIGHEST
            )
            a[pl.ds(k0 + OB, NB - k0 - OB), :] -= update[k0 + OB - lo:]


def factor_kernel(at_ref, own_ref, other_ref, shift_ref, chol_ref, msg_ref, lead, a):
    p, q = at_ref[0], at_ref[1]
    core = q % 2
    lead[pl.ds(pl.multiple_of(core * SHARD, SHARD), SHARD), :] = own_ref[...]
    lead[pl.ds(pl.multiple_of((1 - core) * SHARD, SHARD), SHARD), :] = other_ref[...]
    row = lax.broadcasted_iota(jnp.int32, (NB, NB), 0)
    col = lax.broadcasted_iota(jnp.int32, (NB, NB), 1)
    f0 = lead[...]
    a[:, :NB] = dot(f0, f0, NT) + jnp.where(row == col, shift_ref[...], 0.0)
    a[:, NB:] = jnp.where(row == col, 1.0, 0.0)
    factor_rows(a)
    chol_ref[...] = jnp.where(col >= row, a[:, :NB], 0.0)
    keep = (p == 0) & (q < 2)
    msg_ref[:, :R] = jnp.where(keep, own_ref[...], jnp.zeros_like(own_ref))
    whi, wlo = split(a[:, NB:])
    part = jnp.where(keep, jnp.where(core == 0, whi, wlo), jnp.zeros_like(whi))
    msg_ref[:, R:R + 128] = part[:128, :128]
    msg_ref[:, R + 128:R + 384] = part[128:, :]


def factor(at, own, other, shift):
    vm = pl.BlockSpec(memory_space=pltpu.VMEM)
    return pl.pallas_call(
        factor_kernel,
        out_shape=[jax.ShapeDtypeStruct((NB, NB), f32), jax.ShapeDtypeStruct((SHARD, MSG), bf16)],
        in_specs=[pl.BlockSpec(memory_space=pltpu.SMEM), vm, vm, vm],
        out_specs=[vm, vm],
        scratch_shapes=[pltpu.VMEM((NB, R), bf16), pltpu.VMEM((NB, 2 * NB), f32)],
        compiler_params=pltpu.CompilerParams(vmem_limit_bytes=32 << 20),
        cost_estimate=pl.CostEstimate(flops=20_000_000_000, bytes_accessed=1 << 20, transcendentals=0),
    )(at, own, other, shift)


def tail_kernel(at_ref, *refs):
    mine, theirs, cols = refs[0:4], refs[4:8], refs[8:12]
    lead_ref, other_ref, shift_ref, chol_ref, out_ref, f, a, hhi, hlo, f0, w, ghi_ref, glo_ref, stage, sem = refs[12:]
    p, q = at_ref[0], at_ref[1]
    y, zh = p // 2, p % 2
    zl, x, core = q // 8, q // 2 % 4, q % 2
    g = pl.program_id(0)

    def shard(n):
        return pl.ds(pl.multiple_of(n * SHARD, SHARD), SHARD)

    @pl.when(g == 0)
    def _():
        for n, d in enumerate((0, 1, 3, 2)):
            for j in range(2):
                for bufs, whose in ((mine, core), (theirs, 1 - core)):
                    tile = (zl + j) % 2 * 4 + (x + 4 - d) % 4
                    f[shard(tile * 2 + whose), :] = bufs[n][j]
                a[shard((y + 4 - d) % 4 * 2 + (zh + j) % 2), :] = cols[n][j]
        f0[pl.ds(pl.multiple_of(core * SHARD, SHARD), SHARD), :] = lead_ref[:, :R]
        f0[pl.ds(pl.multiple_of((1 - core) * SHARD, SHARD), SHARD), :] = other_ref[:, :R]
        for n, (own, other) in enumerate(((lead_ref, other_ref), (other_ref, lead_ref))):
            part = jnp.where(core == 0, own[:, R:], other[:, R:])
            w[n, :128, :128] = part[:, :128]
            w[n, :128, 128:] = jnp.zeros((128, 128), bf16)
            w[n, 128:, :] = part[:, 128:]
        ghi, glo = split(dot(w[0], f0[...], NN) + dot(w[1], f0[...], NN))
        ghi_ref[...] = ghi
        glo_ref[...] = glo
        lhi, llo = split(dot(a[...], ghi_ref[...], NT) + dot(a[...], glo_ref[...], NT))
        for k in range(4):
            at = pl.ds(k * NB, NB)
            h = a[:, at].astype(f32) - (
                dot(lhi, ghi_ref[:, at], NN) + dot(lhi, glo_ref[:, at], NN) + dot(llo, ghi_ref[:, at], NN)
            )
            hi, lo = split(h)
            hhi[:, at] = hi
            hlo[:, at] = lo

        @pl.when(q == 0)
        def _():
            hhi[pl.ds(0, NB), :] = ghi_ref[...]
            hlo[pl.ds(0, NB), :] = glo_ref[...]

    def puts(step, slot):
        return [
            pltpu.make_async_copy(
                stage.at[slot, :, pl.ds(c * 128, 128)],
                out_ref.at[pl.ds(pl.multiple_of(step * MB, MB), MB), c, :],
                sem.at[slot, c],
            )
            for c in range(8)
        ]

    slot = g % 2

    @pl.when(g >= 2)
    def _():
        for copy in puts(g - 2, slot):
            copy.wait()

    ft = f[pl.ds(pl.multiple_of(g * MB, MB), MB), :]
    for c in range(4):
        at = pl.ds(c * NB, NB)
        stage[slot, :, at] = dot(ft, hhi[at, :], NT) + dot(ft, hlo[at, :], NT)

    @pl.when((g == 0) & (p == 0))
    def _():
        for c in range(4):
            at = pl.ds(c * NB, NB)
            stage[0, :NB, at] = dot(f[:NB, :], a[at, :], NT)

    row = lax.broadcasted_iota(jnp.int32, (NB, NB), 0)
    col = lax.broadcasted_iota(jnp.int32, (NB, NB), 1)
    for t in range(MB // NB):
        r = g * (MB // NB) + t
        for c in range(4):
            @pl.when((p == q % 8) & (r == 2 * c + q // 8))
            def _():
                shift = shift_ref[pl.ds(r, 1), :]
                stage[slot, t * NB:t * NB + NB, c * NB:c * NB + NB] += jnp.where(row == col, shift, 0.0)

    @pl.when((g == 0) & (p == 0) & (q == 0))
    def _():
        stage[0, :NB, :NB] = chol_ref[...].T

    for copy in puts(g, slot):
        copy.start()

    @pl.when(g == STEPS - 1)
    def _():
        for copy in puts(g - 1, 1 - slot):
            copy.wait()
        for copy in puts(g, slot):
            copy.wait()


def tail(at, mine, theirs, cols, lead, other, shift, chol):
    vm = pl.BlockSpec(memory_space=pltpu.VMEM)
    return pl.pallas_call(
        tail_kernel,
        grid=(STEPS,),
        out_shape=jax.ShapeDtypeStruct((TILES * NB, 8, 128), f32),
        in_specs=[pl.BlockSpec(memory_space=pltpu.SMEM)] + [vm] * 16,
        out_specs=pl.BlockSpec(memory_space=pl.ANY),
        scratch_shapes=[
            pltpu.VMEM((TILES * NB, R), bf16),
            pltpu.VMEM((4 * NB, R), bf16),
            pltpu.VMEM((4 * NB, R), bf16),
            pltpu.VMEM((4 * NB, R), bf16),
            pltpu.VMEM((NB, R), bf16),
            pltpu.VMEM((2, NB, NB), bf16),
            pltpu.VMEM((NB, R), bf16),
            pltpu.VMEM((NB, R), bf16),
            pltpu.VMEM((2, MB, 4 * NB), f32),
            pltpu.SemaphoreType.DMA((2, 8)),
        ],
        compiler_params=pltpu.CompilerParams(vmem_limit_bytes=48 << 20),
    )(at, *mine, *theirs, *cols, lead, other, shift, chol)


def local(factors, shift):
    both = ("prow", "pcol")
    p = lax.axis_index("prow")
    q = lax.axis_index("pcol")
    core = q % 2
    own = factors[0]

    def send(value, pairs):
        return lax.ppermute(value, both, pairs)

    def after(value, *others):
        return lax.optimization_barrier((value, *others))[0]

    at = jnp.stack([p, q])
    to_core = moves(swap_core)

    def spread(lead, pairs):
        a, b, c = [send(lead, to) for to in pairs]
        return lead + (a + b + c)

    def star(piece, axis):
        return [piece] + [send(piece, moves(lambda at: hop(at, axis, d))) for d in (1, 3, 2)]

    rounds = spread_rounds()
    chol, lead = factor(at, own, send(own, to_core), shift[:, :NB])
    piece = send(own, to_columns())
    mine = star(jnp.stack([own, send(own, moves(swap_zl))]), "x")
    lead, piece, mine[1], mine[2] = lax.optimization_barrier((lead, piece, mine[1], mine[2]))
    pair = jnp.stack([piece, send(piece, moves(swap_zh))])
    lead, pair = lax.optimization_barrier((spread(lead, rounds[0]), pair))
    cols = star(pair, "y")
    lead = spread(lead, rounds[1])
    lead, *mine = lax.optimization_barrier((lead, *mine))
    theirs = [send(value, to_core) for value in mine]
    lead, *cols = lax.optimization_barrier((spread(lead, rounds[2]), *cols))
    out = tail(at, mine, theirs, cols, lead, send(lead, to_core), shift.reshape(TILES, NB), chol)
    return out.reshape(1, TILES * NB, 1, 4 * NB)


def solution(mesh):
    in_specs = (P("prow", "pcol", None), P("prow", None))
    out_specs = P("prow", None, "pcol", None)
    return jax.shard_map(local, mesh=mesh, in_specs=in_specs, out_specs=out_specs, check_vma=False)
```

time: 113 us -> 107 us (0.947)
  the two profiles are of different devices: /device:TPU:31 before, /device:TPU:1 now
where the time goes in v2:
time: 107 us
  starting transfers between devices  39.3 us (37%)
  waiting for transfers between devices  30.6 us (29%)
  Pallas kernels  29.9 us (28%)
  local copies, waits for them, and re-layouts  4.6 us (4%)
  other arithmetic  1.93 us (2%)
    ppermute x24, starting transfers between devices, send(): return lax.ppermute(value, both, pairs)  39.3 us
    ppermute x24, waiting for transfers between devices, send(): return lax.ppermute(value, both, pairs)  30.6 us
    pallas_call x1, Pallas kernels, tail(): pl.pallas_call(tail_kernel, grid=(STEPS,), out_shape=jax.ShapeDtypeStruct...  19.5 us
    pallas_call x1, Pallas kernels, factor(): pl.pallas_call(factor_kernel, out_shape=[jax.ShapeDtypeStruct((NB, NB), f...  10.4 us
    unnamed x15, local copies, waits for them, and re-layouts  3.92 us
  transfers between devices with their start and end apart: 24, of which 11 were waited for; matrix products, arithmetic and copies ran while one was open for 3% of the time, Pallas kernels for 10%

profile of v2, /device:TPU:1, one launch (start us, length us, event | category | flops | bytes accessed | tf_op | source)
XLA Modules:
  0.0 106.7 jit_solution(1543501345590067000)
XLA Ops:
  0.0 2.5 %collective-permute-start.2 = (bf16[128,1024]{1,0:T(8,128)(2,1)}, bf16[128,1024]{1,0:T(8,128)(2,1)S(1)}, u32[]{:S(2)}, u32[]{:S(2)}) collective-permute-start(bf16[128,1024]{1,0:T(8,128)(2,1)} %bitcast.7), channel_id=1, source_target_pairs={{0,8},{1,9},{2,10},{3,11},{4,12},{5,13},{6,14},{7,15},{8,0},{9,1},... | collective-permute-start | bytes 786440 | tf_op jit(solution)/shard_map/ppermute | solution.py:303
  3.4 5.1 %collective-permute-start.1 = (bf16[128,1024]{1,0:T(8,128)(2,1)}, bf16[128,1024]{1,0:T(8,128)(2,1)S(1)}, u32[]{:S(2)}, u32[]{:S(2)}) collective-permute-start(bf16[128,1024]{1,0:T(8,128)(2,1)} %bitcast.9), channel_id=1, source_target_pairs={{0,0},{1,16},{2,8},{3,24},{4,32},{5,48},{6,40},{7,56},{8,64},{9,80... | collective-permute-start | bytes 786440 | tf_op jit(solution)/shard_map/ppermute | solution.py:303
  10.7 2.1 %collective-permute-start.4 = (bf16[2,128,1024]{2,1,0:T(8,128)(2,1)S(1)}, bf16[2,128,1024]{2,1,0:T(8,128)(2,1)S(1)}, u32[]{:S(2)}, u32[]{:S(2)}) collective-permute-start(bf16[2,128,1024]{2,1,0:T(8,128)(2,1)S(1)} %pad_maximum_fusion.refs_0_), channel_id=1, source_target_pairs={{0,6},{1,7},{2,0},{3,1},{4,2},{5,3},{6,4},{7,5},{8,14},{9,15},{10,... | collective-permute-start | bytes 1572872 | tf_op jit(solution)/shard_map/ppermute | solution.py:303
  13.7 10.4 %shard_map.28 = (f32[256,256]{1,0:T(8,128)S(1)}, bf16[128,1408]{1,0:T(8,128)(2,1)S(1)}) custom-call(s32[2]{0:T(128)S(1)} %pad_add_fusion.at_ref, bf16[128,1024]{1,0:T(8,128)(2,1)S(1)} %bitcast.10, bf16[128,1024]{1,0:T(8,128)(2,1)S(1)} %collective-permute-done.other_ref, f32[1,256]{1,0:T(1,128)S(1)} %slice.3.shift_ref), custom_call_target="tpu_custom_call" | custom-call | flops 20000000000 | bytes 1048576 | tf_op jit(solution)/shard_map/pallas_call | solution.py:163
  24.8 7.8 %collective-permute-done.3.refs_1_ = bf16[2,128,1024]{2,1,0:T(8,128)(2,1)S(1)} collective-permute-done((bf16[2,128,1024]{2,1,0:T(8,128)(2,1)S(1)}, bf16[2,128,1024]{2,1,0:T(8,128)(2,1)S(1)}, u32[]{:S(2)}, u32[]{:S(2)}) %collective-permute-start.3) | collective-permute-done | bytes 524320 | tf_op jit(solution)/shard_map/ppermute | solution.py:303
  32.6 2.3 %collective-permute-start.8 = (bf16[128,1024]{1,0:T(8,128)(2,1)S(1)}, bf16[128,1024]{1,0:T(8,128)(2,1)S(1)}, u32[]{:S(2)}, u32[]{:S(2)}) collective-permute-start(bf16[128,1024]{1,0:T(8,128)(2,1)S(1)} %collective-permute-done.1), channel_id=1, source_target_pairs={{0,16},{1,17},{2,18},{3,19},{4,20},{5,21},{6,22},{7,23},{8,24},{9,... | collective-permute-start | bytes 786440 | tf_op jit(solution)/shard_map/ppermute | solution.py:303
  36.2 2.0 %collective-permute-start.6 = (bf16[128,1408]{1,0:T(8,128)(2,1)S(1)}, bf16[128,1408]{1,0:T(8,128)(2,1)S(1)}, u32[]{:S(2)}, u32[]{:S(2)}) collective-permute-start(bf16[128,1408]{1,0:T(8,128)(2,1)S(1)} %get-tuple-element.24), channel_id=1, source_target_pairs={{0,6},{1,97}} | collective-permute-start | bytes 1081352 | tf_op jit(solution)/shard_map/ppermute | solution.py:303
  39.6 2.6 %collective-permute-done.8 = bf16[128,1024]{1,0:T(8,128)(2,1)S(1)} collective-permute-done((bf16[128,1024]{1,0:T(8,128)(2,1)S(1)}, bf16[128,1024]{1,0:T(8,128)(2,1)S(1)}, u32[]{:S(2)}, u32[]{:S(2)}) %collective-permute-start.8) | collective-permute-done | bytes 262176 | tf_op jit(solution)/shard_map/ppermute | solution.py:303
  42.6 1.8 %collective-permute-done.5 = bf16[128,1408]{1,0:T(8,128)(2,1)S(1)} collective-permute-done((bf16[128,1408]{1,0:T(8,128)(2,1)S(1)}, bf16[128,1408]{1,0:T(8,128)(2,1)S(1)}, u32[]{:S(2)}, u32[]{:S(2)}) %collective-permute-start.5) | collective-permute-done | bytes 360480 | tf_op jit(solution)/shard_map/ppermute | solution.py:303
  44.5 2.0 %collective-permute-start.11 = (bf16[128,1408]{1,0:T(8,128)(2,1)S(1)}, bf16[128,1408]{1,0:T(8,128)(2,1)S(1)}, u32[]{:S(2)}, u32[]{:S(2)}) collective-permute-start(bf16[128,1408]{1,0:T(8,128)(2,1)S(1)} %add_add_fusion.2), channel_id=1, source_target_pairs={{0,64},{2,66},{6,70},{4,68},{1,17},{33,49},{97,113},{65,81}} | collective-permute-start | bytes 1081352 | tf_op jit(solution)/shard_map/ppermute | solution.py:303
  46.5 1.3 %collective-permute-start.10 = (bf16[128,1408]{1,0:T(8,128)(2,1)S(1)}, bf16[128,1408]{1,0:T(8,128)(2,1)S(1)}, u32[]{:S(2)}, u32[]{:S(2)}) collective-permute-start(bf16[128,1408]{1,0:T(8,128)(2,1)S(1)} %add_add_fusion.2), channel_id=1, source_target_pairs={{0,96},{2,98},{6,102},{4,100},{1,25},{33,57},{97,121},{65,89}} | collective-permute-start | bytes 1081352 | tf_op jit(solution)/shard_map/ppermute | solution.py:303
  47.8 1.3 %collective-permute-start.9 = (bf16[128,1408]{1,0:T(8,128)(2,1)S(1)}, bf16[128,1408]{1,0:T(8,128)(2,1)S(1)}, u32[]{:S(2)}, u32[]{:S(2)}) collective-permute-start(bf16[128,1408]{1,0:T(8,128)(2,1)S(1)} %add_add_fusion.2), channel_id=1, source_target_pairs={{0,32},{2,34},{6,38},{4,36},{1,9},{33,41},{97,105},{65,73}} | collective-permute-start | bytes 1081352 | tf_op jit(solution)/shard_map/ppermute | solution.py:303
  49.4 1.5 %collective-permute-done.11 = bf16[128,1408]{1,0:T(8,128)(2,1)S(1)} collective-permute-done((bf16[128,1408]{1,0:T(8,128)(2,1)S(1)}, bf16[128,1408]{1,0:T(8,128)(2,1)S(1)}, u32[]{:S(2)}, u32[]{:S(2)}) %collective-permute-start.11) | collective-permute-done | bytes 360480 | tf_op jit(solution)/shard_map/ppermute | solution.py:303
  50.9 2.1 %collective-permute-start.21 = (bf16[2,128,1024]{2,1,0:T(8,128)(2,1)S(1)}, bf16[2,128,1024]{2,1,0:T(8,128)(2,1)S(1)}, u32[]{:S(2)}, u32[]{:S(2)}) collective-permute-start(bf16[2,128,1024]{2,1,0:T(8,128)(2,1)S(1)} %pad_maximum_fusion.1.refs_8_), channel_id=1, source_target_pairs={{0,96},{1,97},{2,98},{3,99},{4,100},{5,101},{6,102},{7,103},{8,104... | collective-permute-start | bytes 1572872 | tf_op jit(solution)/shard_map/ppermute | solution.py:303
  52.9 1.8 %collective-permute-done.9 = bf16[128,1408]{1,0:T(8,128)(2,1)S(1)} collective-permute-done((bf16[128,1408]{1,0:T(8,128)(2,1)S(1)}, bf16[128,1408]{1,0:T(8,128)(2,1)S(1)}, u32[]{:S(2)}, u32[]{:S(2)}) %collective-permute-start.9) | collective-permute-done | bytes 360480 | tf_op jit(solution)/shard_map/ppermute | solution.py:303
  54.8 9.5 %collective-permute-done.12.refs_3_ = bf16[2,128,1024]{2,1,0:T(8,128)(2,1)S(1)} collective-permute-done((bf16[2,128,1024]{2,1,0:T(8,128)(2,1)S(1)}, bf16[2,128,1024]{2,1,0:T(8,128)(2,1)S(1)}, u32[]{:S(2)}, u32[]{:S(2)}) %collective-permute-start.12) | collective-permute-done | bytes 524320 | tf_op jit(solution)/shard_map/ppermute | solution.py:303
  65.6 1.3 %collective-permute-start.18 = (bf16[128,1408]{1,0:T(8,128)(2,1)S(1)}, bf16[128,1408]{1,0:T(8,128)(2,1)S(1)}, u32[]{:S(2)}, u32[]{:S(2)}) collective-permute-start(bf16[128,1408]{1,0:T(8,128)(2,1)S(1)} %add_add_fusion.1), channel_id=1, source_target_pairs={{0,24},{2,26},{6,30},{4,28},{32,56},{34,58},{38,62},{36,60},{96,12... | collective-permute-start | bytes 1081352 | tf_op jit(solution)/shard_map/ppermute | solution.py:303
  66.9 1.3 %collective-permute-start.17 = (bf16[128,1408]{1,0:T(8,128)(2,1)S(1)}, bf16[128,1408]{1,0:T(8,128)(2,1)S(1)}, u32[]{:S(2)}, u32[]{:S(2)}) collective-permute-start(bf16[128,1408]{1,0:T(8,128)(2,1)S(1)} %add_add_fusion.1), channel_id=1, source_target_pairs={{0,8},{2,10},{6,14},{4,12},{32,40},{34,42},{38,46},{36,44},{96,104... | collective-permute-start | bytes 1081352 | tf_op jit(solution)/shard_map/ppermute | solution.py:303
  68.4 3.1 %collective-permute-done.21.refs_10_ = bf16[2,128,1024]{2,1,0:T(8,128)(2,1)S(1)} collective-permute-done((bf16[2,128,1024]{2,1,0:T(8,128)(2,1)S(1)}, bf16[2,128,1024]{2,1,0:T(8,128)(2,1)S(1)}, u32[]{:S(2)}, u32[]{:S(2)}) %collective-permute-start.21) | collective-permute-done | bytes 524320 | tf_op jit(solution)/shard_map/ppermute | solution.py:303
  71.5 3.5 %collective-permute-start.13 = (bf16[2,128,1024]{2,1,0:T(8,128)(2,1)S(1)}, bf16[2,128,1024]{2,1,0:T(8,128)(2,1)S(1)}, u32[]{:S(2)}, u32[]{:S(2)}) collective-permute-start(bf16[2,128,1024]{2,1,0:T(8,128)(2,1)S(1)} %pad_maximum_fusion.refs_0_), channel_id=1, source_target_pairs={{0,1},{1,0},{2,3},{3,2},{4,5},{5,4},{6,7},{7,6},{8,9},{9,8},{10,11... | collective-permute-start | bytes 1572872 | tf_op jit(solution)/shard_map/ppermute | solution.py:303
  75.5 2.2 %collective-permute-start.16 = (bf16[2,128,1024]{2,1,0:T(8,128)(2,1)S(1)}, bf16[2,128,1024]{2,1,0:T(8,128)(2,1)}, u32[]{:S(2)}, u32[]{:S(2)}) collective-permute-start(bf16[2,128,1024]{2,1,0:T(8,128)(2,1)S(1)} %collective-permute-done.12.refs_3_), channel_id=1, source_target_pairs={{0,1},{1,0},{2,3},{3,2},{4,5},{5,4},{6,7},{7,6},{8,9},{9,8},{10,11... | collective-permute-start | bytes 1572872 | tf_op jit(solution)/shard_map/ppermute | solution.py:303
  77.8 1.4 %collective-permute-done.20.refs_9_ = bf16[2,128,1024]{2,1,0:T(8,128)(2,1)S(1)} collective-permute-done((bf16[2,128,1024]{2,1,0:T(8,128)(2,1)S(1)}, bf16[2,128,1024]{2,1,0:T(8,128)(2,1)S(1)}, u32[]{:S(2)}, u32[]{:S(2)}) %collective-permute-start.20) | collective-permute-done | bytes 524320 | tf_op jit(solution)/shard_map/ppermute | solution.py:303
  80.0 4.7 %collective-permute-start.23 = (bf16[128,1408]{1,0:T(8,128)(2,1)S(1)}, bf16[128,1408]{1,0:T(8,128)(2,1)}, u32[]{:S(2)}, u32[]{:S(2)}) collective-permute-start(bf16[128,1408]{1,0:T(8,128)(2,1)S(1)} %add_add_fusion.refs_12_), channel_id=1, source_target_pairs={{0,1},{1,0},{2,3},{3,2},{4,5},{5,4},{6,7},{7,6},{8,9},{9,8},{10,11... | collective-permute-start | bytes 1081352 | tf_op jit(solution)/shard_map/ppermute | solution.py:303
  87.1 19.5 %shard_map.29 = f32[2048,8,128]{2,1,0:T(8,128)} custom-call(s32[2]{0:T(128)S(1)} %pad_add_fusion.at_ref, bf16[2,128,1024]{2,1,0:T(8,128)(2,1)S(1)} %pad_maximum_fusion.refs_0_, bf16[2,128,1024]{2,1,0:T(8,128)(2,1)S(1)} %collective-permute-done.3.refs_1_, bf16[2,128,1024]{2,1,0:T(8,128)(2,1)S(1)} %collective-permute-done.4.refs_2_, ...), custom_call_target="tpu_custom_call" | custom-call | tf_op jit(solution)/shard_map/pallas_call | solution.py:273
  (50 shorter events, 13.2 us)
Async XLA Ops:
  0.0 9.6 %collective-permute-start.2 = (bf16[128,1024]{1,0:T(8,128)(2,1)}, bf16[128,1024]{1,0:T(8,128)(2,1)S(1)}, u32[]{:S(2)}, u32[]{:S(2)}) collective-permute-start(bf16[128,1024]{1,0:T(8,128)(2,1)} %bitcast.7), channel_id=1, source_target_pairs={{0,8},{1,9},{2,10},{3,11},{4,12},{5,13},{6,14},{7,15},{8,0},{9,1},... | collective-permute-start | bytes 786440 | tf_op jit(solution)/shard_map/ppermute | solution.py:303
  2.5 10.3 %collective-permute-start = (bf16[128,1024]{1,0:T(8,128)(2,1)}, bf16[128,1024]{1,0:T(8,128)(2,1)S(1)}, u32[]{:S(2)}, u32[]{:S(2)}) collective-permute-start(bf16[128,1024]{1,0:T(8,128)(2,1)} %bitcast.8), channel_id=1, source_target_pairs={{0,1},{1,0},{2,3},{3,2},{4,5},{5,4},{6,7},{7,6},{8,9},{9,8},{10,11... | collective-permute-start | bytes 786440 | tf_op jit(solution)/shard_map/ppermute | solution.py:303
  3.4 21.4 %collective-permute-start.1 = (bf16[128,1024]{1,0:T(8,128)(2,1)}, bf16[128,1024]{1,0:T(8,128)(2,1)S(1)}, u32[]{:S(2)}, u32[]{:S(2)}) collective-permute-start(bf16[128,1024]{1,0:T(8,128)(2,1)} %bitcast.9), channel_id=1, source_target_pairs={{0,0},{1,16},{2,8},{3,24},{4,32},{5,48},{6,40},{7,56},{8,64},{9,80... | collective-permute-start | bytes 786440 | tf_op jit(solution)/shard_map/ppermute | solution.py:303
  10.7 14.1 %collective-permute-start.4 = (bf16[2,128,1024]{2,1,0:T(8,128)(2,1)S(1)}, bf16[2,128,1024]{2,1,0:T(8,128)(2,1)S(1)}, u32[]{:S(2)}, u32[]{:S(2)}) collective-permute-start(bf16[2,128,1024]{2,1,0:T(8,128)(2,1)S(1)} %pad_maximum_fusion.refs_0_), channel_id=1, source_target_pairs={{0,6},{1,7},{2,0},{3,1},{4,2},{5,3},{6,4},{7,5},{8,14},{9,15},{10,... | collective-permute-start | bytes 1572872 | tf_op jit(solution)/shard_map/ppermute | solution.py:303
  12.7 19.9 %collective-permute-start.3 = (bf16[2,128,1024]{2,1,0:T(8,128)(2,1)S(1)}, bf16[2,128,1024]{2,1,0:T(8,128)(2,1)S(1)}, u32[]{:S(2)}, u32[]{:S(2)}) collective-permute-start(bf16[2,128,1024]{2,1,0:T(8,128)(2,1)S(1)} %pad_maximum_fusion.refs_0_), channel_id=1, source_target_pairs={{0,2},{1,3},{2,4},{3,5},{4,6},{5,7},{6,0},{7,1},{8,10},{9,11},{10,... | collective-permute-start | bytes 1572872 | tf_op jit(solution)/shard_map/ppermute | solution.py:303
  32.6 9.6 %collective-permute-start.8 = (bf16[128,1024]{1,0:T(8,128)(2,1)S(1)}, bf16[128,1024]{1,0:T(8,128)(2,1)S(1)}, u32[]{:S(2)}, u32[]{:S(2)}) collective-permute-start(bf16[128,1024]{1,0:T(8,128)(2,1)S(1)} %collective-permute-done.1), channel_id=1, source_target_pairs={{0,16},{1,17},{2,18},{3,19},{4,20},{5,21},{6,22},{7,23},{8,24},{9,... | collective-permute-start | bytes 786440 | tf_op jit(solution)/shard_map/ppermute | solution.py:303
  34.9 7.4 %collective-permute-start.7 = (bf16[128,1408]{1,0:T(8,128)(2,1)S(1)}, bf16[128,1408]{1,0:T(8,128)(2,1)S(1)}, u32[]{:S(2)}, u32[]{:S(2)}) collective-permute-start(bf16[128,1408]{1,0:T(8,128)(2,1)S(1)} %get-tuple-element.24), channel_id=1, source_target_pairs={{0,4},{1,65}} | collective-permute-start | bytes 1081352 | tf_op jit(solution)/shard_map/ppermute | solution.py:303
  36.2 6.4 %collective-permute-start.6 = (bf16[128,1408]{1,0:T(8,128)(2,1)S(1)}, bf16[128,1408]{1,0:T(8,128)(2,1)S(1)}, u32[]{:S(2)}, u32[]{:S(2)}) collective-permute-start(bf16[128,1408]{1,0:T(8,128)(2,1)S(1)} %get-tuple-element.24), channel_id=1, source_target_pairs={{0,6},{1,97}} | collective-permute-start | bytes 1081352 | tf_op jit(solution)/shard_map/ppermute | solution.py:303
  38.3 6.1 %collective-permute-start.5 = (bf16[128,1408]{1,0:T(8,128)(2,1)S(1)}, bf16[128,1408]{1,0:T(8,128)(2,1)S(1)}, u32[]{:S(2)}, u32[]{:S(2)}) collective-permute-start(bf16[128,1408]{1,0:T(8,128)(2,1)S(1)} %get-tuple-element.24), channel_id=1, source_target_pairs={{0,2},{1,33}} | collective-permute-start | bytes 1081352 | tf_op jit(solution)/shard_map/ppermute | solution.py:303
  44.5 6.4 %collective-permute-start.11 = (bf16[128,1408]{1,0:T(8,128)(2,1)S(1)}, bf16[128,1408]{1,0:T(8,128)(2,1)S(1)}, u32[]{:S(2)}, u32[]{:S(2)}) collective-permute-start(bf16[128,1408]{1,0:T(8,128)(2,1)S(1)} %add_add_fusion.2), channel_id=1, source_target_pairs={{0,64},{2,66},{6,70},{4,68},{1,17},{33,49},{97,113},{65,81}} | collective-permute-start | bytes 1081352 | tf_op jit(solution)/shard_map/ppermute | solution.py:303
  46.5 6.4 %collective-permute-start.10 = (bf16[128,1408]{1,0:T(8,128)(2,1)S(1)}, bf16[128,1408]{1,0:T(8,128)(2,1)S(1)}, u32[]{:S(2)}, u32[]{:S(2)}) collective-permute-start(bf16[128,1408]{1,0:T(8,128)(2,1)S(1)} %add_add_fusion.2), channel_id=1, source_target_pairs={{0,96},{2,98},{6,102},{4,100},{1,25},{33,57},{97,121},{65,89}} | collective-permute-start | bytes 1081352 | tf_op jit(solution)/shard_map/ppermute | solution.py:303
  47.8 6.9 %collective-permute-start.9 = (bf16[128,1408]{1,0:T(8,128)(2,1)S(1)}, bf16[128,1408]{1,0:T(8,128)(2,1)S(1)}, u32[]{:S(2)}, u32[]{:S(2)}) collective-permute-start(bf16[128,1408]{1,0:T(8,128)(2,1)S(1)} %add_add_fusion.2), channel_id=1, source_target_pairs={{0,32},{2,34},{6,38},{4,36},{1,9},{33,41},{97,105},{65,73}} | collective-permute-start | bytes 1081352 | tf_op jit(solution)/shard_map/ppermute | solution.py:303
  49.2 15.1 %collective-permute-start.12 = (bf16[2,128,1024]{2,1,0:T(8,128)(2,1)S(1)}, bf16[2,128,1024]{2,1,0:T(8,128)(2,1)S(1)}, u32[]{:S(2)}, u32[]{:S(2)}) collective-permute-start(bf16[2,128,1024]{2,1,0:T(8,128)(2,1)S(1)} %pad_maximum_fusion.refs_0_), channel_id=1, source_target_pairs={{0,4},{1,5},{2,6},{3,7},{4,0},{5,1},{6,2},{7,3},{8,12},{9,13},{10,... | collective-permute-start | bytes 1572872 | tf_op jit(solution)/shard_map/ppermute | solution.py:303
  49.3 19.0 %collective-permute-start.22 = (bf16[2,128,1024]{2,1,0:T(8,128)(2,1)S(1)}, bf16[2,128,1024]{2,1,0:T(8,128)(2,1)S(1)}, u32[]{:S(2)}, u32[]{:S(2)}) collective-permute-start(bf16[2,128,1024]{2,1,0:T(8,128)(2,1)S(1)} %pad_maximum_fusion.1.refs_8_), channel_id=1, source_target_pairs={{0,64},{1,65},{2,66},{3,67},{4,68},{5,69},{6,70},{7,71},{8,72},{9,... | collective-permute-start | bytes 1572872 | tf_op jit(solution)/shard_map/ppermute | solution.py:303
  50.9 20.7 %collective-permute-start.21 = (bf16[2,128,1024]{2,1,0:T(8,128)(2,1)S(1)}, bf16[2,128,1024]{2,1,0:T(8,128)(2,1)S(1)}, u32[]{:S(2)}, u32[]{:S(2)}) collective-permute-start(bf16[2,128,1024]{2,1,0:T(8,128)(2,1)S(1)} %pad_maximum_fusion.1.refs_8_), channel_id=1, source_target_pairs={{0,96},{1,97},{2,98},{3,99},{4,100},{5,101},{6,102},{7,103},{8,104... | collective-permute-start | bytes 1572872 | tf_op jit(solution)/shard_map/ppermute | solution.py:303
  64.3 10.7 %collective-permute-start.19 = (bf16[128,1408]{1,0:T(8,128)(2,1)S(1)}, bf16[128,1408]{1,0:T(8,128)(2,1)S(1)}, u32[]{:S(2)}, u32[]{:S(2)}) collective-permute-start(bf16[128,1408]{1,0:T(8,128)(2,1)S(1)} %add_add_fusion.1), channel_id=1, source_target_pairs={{0,16},{2,18},{6,22},{4,20},{32,48},{34,50},{38,54},{36,52},{96,11... | collective-permute-start | bytes 1081352 | tf_op jit(solution)/shard_map/ppermute | solution.py:303
  65.6 9.5 %collective-permute-start.18 = (bf16[128,1408]{1,0:T(8,128)(2,1)S(1)}, bf16[128,1408]{1,0:T(8,128)(2,1)S(1)}, u32[]{:S(2)}, u32[]{:S(2)}) collective-permute-start(bf16[128,1408]{1,0:T(8,128)(2,1)S(1)} %add_add_fusion.1), channel_id=1, source_target_pairs={{0,24},{2,26},{6,30},{4,28},{32,56},{34,58},{38,62},{36,60},{96,12... | collective-permute-start | bytes 1081352 | tf_op jit(solution)/shard_map/ppermute | solution.py:303
  66.9 8.6 %collective-permute-start.17 = (bf16[128,1408]{1,0:T(8,128)(2,1)S(1)}, bf16[128,1408]{1,0:T(8,128)(2,1)S(1)}, u32[]{:S(2)}, u32[]{:S(2)}) collective-permute-start(bf16[128,1408]{1,0:T(8,128)(2,1)S(1)} %add_add_fusion.1), channel_id=1, source_target_pairs={{0,8},{2,10},{6,14},{4,12},{32,40},{34,42},{38,46},{36,44},{96,104... | collective-permute-start | bytes 1081352 | tf_op jit(solution)/shard_map/ppermute | solution.py:303
  68.3 10.9 %collective-permute-start.20 = (bf16[2,128,1024]{2,1,0:T(8,128)(2,1)S(1)}, bf16[2,128,1024]{2,1,0:T(8,128)(2,1)S(1)}, u32[]{:S(2)}, u32[]{:S(2)}) collective-permute-start(bf16[2,128,1024]{2,1,0:T(8,128)(2,1)S(1)} %pad_maximum_fusion.1.refs_8_), channel_id=1, source_target_pairs={{0,32},{1,33},{2,34},{3,35},{4,36},{5,37},{6,38},{7,39},{8,40},{9,... | collective-permute-start | bytes 1572872 | tf_op jit(solution)/shard_map/ppermute | solution.py:303
  71.5 14.3 %collective-permute-start.13 = (bf16[2,128,1024]{2,1,0:T(8,128)(2,1)S(1)}, bf16[2,128,1024]{2,1,0:T(8,128)(2,1)S(1)}, u32[]{:S(2)}, u32[]{:S(2)}) collective-permute-start(bf16[2,128,1024]{2,1,0:T(8,128)(2,1)S(1)} %pad_maximum_fusion.refs_0_), channel_id=1, source_target_pairs={{0,1},{1,0},{2,3},{3,2},{4,5},{5,4},{6,7},{7,6},{8,9},{9,8},{10,11... | collective-permute-start | bytes 1572872 | tf_op jit(solution)/shard_map/ppermute | solution.py:303
  75.0 10.8 %collective-permute-start.14 = (bf16[2,128,1024]{2,1,0:T(8,128)(2,1)S(1)}, bf16[2,128,1024]{2,1,0:T(8,128)(2,1)}, u32[]{:S(2)}, u32[]{:S(2)}) collective-permute-start(bf16[2,128,1024]{2,1,0:T(8,128)(2,1)S(1)} %collective-permute-done.3.refs_1_), channel_id=1, source_target_pairs={{0,1},{1,0},{2,3},{3,2},{4,5},{5,4},{6,7},{7,6},{8,9},{9,8},{10,11... | collective-permute-start | bytes 1572872 | tf_op jit(solution)/shard_map/ppermute | solution.py:303
  75.1 10.8 %collective-permute-start.15 = (bf16[2,128,1024]{2,1,0:T(8,128)(2,1)S(1)}, bf16[2,128,1024]{2,1,0:T(8,128)(2,1)}, u32[]{:S(2)}, u32[]{:S(2)}) collective-permute-start(bf16[2,128,1024]{2,1,0:T(8,128)(2,1)S(1)} %collective-permute-done.4.refs_2_), channel_id=1, source_target_pairs={{0,1},{1,0},{2,3},{3,2},{4,5},{5,4},{6,7},{7,6},{8,9},{9,8},{10,11... | collective-permute-start | bytes 1572872 | tf_op jit(solution)/shard_map/ppermute | solution.py:303
  75.5 10.3 %collective-permute-start.16 = (bf16[2,128,1024]{2,1,0:T(8,128)(2,1)S(1)}, bf16[2,128,1024]{2,1,0:T(8,128)(2,1)}, u32[]{:S(2)}, u32[]{:S(2)}) collective-permute-start(bf16[2,128,1024]{2,1,0:T(8,128)(2,1)S(1)} %collective-permute-done.12.refs_3_), channel_id=1, source_target_pairs={{0,1},{1,0},{2,3},{3,2},{4,5},{5,4},{6,7},{7,6},{8,9},{9,8},{10,11... | collective-permute-start | bytes 1572872 | tf_op jit(solution)/shard_map/ppermute | solution.py:303
  80.0 6.1 %collective-permute-start.23 = (bf16[128,1408]{1,0:T(8,128)(2,1)S(1)}, bf16[128,1408]{1,0:T(8,128)(2,1)}, u32[]{:S(2)}, u32[]{:S(2)}) collective-permute-start(bf16[128,1408]{1,0:T(8,128)(2,1)S(1)} %add_add_fusion.refs_12_), channel_id=1, source_target_pairs={{0,1},{1,0},{2,3},{3,2},{4,5},{5,4},{6,7},{7,6},{8,9},{9,8},{10,11... | collective-permute-start | bytes 1081352 | tf_op jit(solution)/shard_map/ppermute | solution.py:303
  (7 other events, 97.6 us)

commit v3 on v2

--- a/solution.py
+++ b/solution.py
@@ -146,7 +146,7 @@
     row = lax.broadcasted_iota(jnp.int32, (NB, NB), 0)
     col = lax.broadcasted_iota(jnp.int32, (NB, NB), 1)
     f0 = lead[...]
-    a[:, :NB] = dot(f0, f0, NT) + jnp.where(row == col, shift_ref[...], 0.0)
+    a[:, :NB] = dot(f0, f0, NT) + jnp.where(row == col, shift_ref[:, :NB], 0.0)
     a[:, NB:] = jnp.where(row == col, 1.0, 0.0)
     factor_rows(a)
     chol_ref[...] = jnp.where(col >= row, a[:, :NB], 0.0)
@@ -250,7 +250,7 @@
         for c in range(4):
             @pl.when((p == q % 8) & (r == 2 * c + q // 8))
             def _():
-                shift = shift_ref[pl.ds(r, 1), :]
+                shift = shift_ref[:, pl.ds(pl.multiple_of(r * NB, NB), NB)]
                 stage[slot, t * NB:t * NB + NB, c * NB:c * NB + NB] += jnp.where(row == col, shift, 0.0)
 
     @pl.when((g == 0) & (p == 0) & (q == 0))
@@ -316,7 +316,7 @@
         return [piece] + [send(piece, moves(lambda at: hop(at, axis, d))) for d in (1, 3, 2)]
 
     rounds = spread_rounds()
-    chol, lead = factor(at, own, send(own, to_core), shift[:, :NB])
+    chol, lead = factor(at, own, send(own, to_core), shift)
     piece = send(own, to_columns())
     mine = star(jnp.stack([own, send(own, moves(swap_zl))]), "x")
     lead, piece, mine[1], mine[2] = lax.optimization_barrier((lead, piece, mine[1], mine[2]))
@@ -327,7 +327,7 @@
     lead, *mine = lax.optimization_barrier((lead, *mine))
     theirs = [send(value, to_core) for value in mine]
     lead, *cols = lax.optimization_barrier((spread(lead, rounds[2]), *cols))
-    out = tail(at, mine, theirs, cols, lead, send(lead, to_core), shift.reshape(TILES, NB), chol)
+    out = tail(at, mine, theirs, cols, lead, send(lead, to_core), shift, chol)
     return out.reshape(1, TILES * NB, 1, 4 * NB)
 
 

time: 107 us -> 105 us (0.981)
  local copies, waits for them, and re-layouts: 4.6 us -> 1.66 us
  waiting for transfers between devices: 30.6 us -> 32.7 us
    unnamed x15 -> x12, local copies, waits for them, and re-layouts: 3.92 us -> 1.66 us
    ppermute x24, waiting for transfers between devices: 30.6 us -> 32.7 us  [send(): return lax.ppermute(value, both, pairs)]
  transfers between devices with their start and end apart: 24 -> 24, of which waited for: 11 -> 11; matrix products, arithmetic and copies ran while one was open for 3% -> 1% of each run, Pallas kernels for 10% -> 10%
where the time goes in v3:
time: 105 us; the launch traced here: 104 us
  starting transfers between devices  38.8 us (37%)
  waiting for transfers between devices  32.7 us (31%)
  Pallas kernels  29.4 us (28%)
  local copies, waits for them, and re-layouts  1.66 us (2%)
  other arithmetic  1.39 us (1%)
    ppermute x24, starting transfers between devices, send(): return lax.ppermute(value, both, pairs)  38.8 us
    ppermute x24, waiting for transfers between devices, send(): return lax.ppermute(value, both, pairs)  32.7 us
    pallas_call x1, Pallas kernels, tail(): pl.pallas_call(tail_kernel, grid=(STEPS,), out_shape=jax.ShapeDtypeStruct...  19 us
    pallas_call x1, Pallas kernels, factor(): pl.pallas_call(factor_kernel, out_shape=[jax.ShapeDtypeStruct((NB, NB), f...  10.4 us
  transfers between devices with their start and end apart: 24, of which 11 were waited for; matrix products, arithmetic and copies ran while one was open for 1% of the time, Pallas kernels for 10%

profile of v3, /device:TPU:1, one launch (start us, length us, event | category | flops | bytes accessed | tf_op | source)
XLA Modules:
  0.0 104.3 jit_solution(7385690427184698065)
XLA Ops:
  0.0 2.5 %collective-permute-start.2 = (bf16[128,1024]{1,0:T(8,128)(2,1)}, bf16[128,1024]{1,0:T(8,128)(2,1)S(1)}, u32[]{:S(2)}, u32[]{:S(2)}) collective-permute-start(bf16[128,1024]{1,0:T(8,128)(2,1)} %bitcast.7), channel_id=1, source_target_pairs={{0,8},{1,9},{2,10},{3,11},{4,12},{5,13},{6,14},{7,15},{8,0},{9,1},... | collective-permute-start | bytes 786440 | tf_op jit(solution)/shard_map/ppermute | solution.py:303
  3.4 5.1 %collective-permute-start.1 = (bf16[128,1024]{1,0:T(8,128)(2,1)}, bf16[128,1024]{1,0:T(8,128)(2,1)S(1)}, u32[]{:S(2)}, u32[]{:S(2)}) collective-permute-start(bf16[128,1024]{1,0:T(8,128)(2,1)} %bitcast.9), channel_id=1, source_target_pairs={{0,0},{1,16},{2,8},{3,24},{4,32},{5,48},{6,40},{7,56},{8,64},{9,80... | collective-permute-start | bytes 786440 | tf_op jit(solution)/shard_map/ppermute | solution.py:303
  10.7 1.5 %collective-permute-start.4 = (bf16[2,128,1024]{2,1,0:T(8,128)(2,1)S(1)}, bf16[2,128,1024]{2,1,0:T(8,128)(2,1)S(1)}, u32[]{:S(2)}, u32[]{:S(2)}) collective-permute-start(bf16[2,128,1024]{2,1,0:T(8,128)(2,1)S(1)} %pad_maximum_fusion.refs_0_), channel_id=1, source_target_pairs={{0,6},{1,7},{2,0},{3,1},{4,2},{5,3},{6,4},{7,5},{8,14},{9,15},{10,... | collective-permute-start | bytes 1572872 | tf_op jit(solution)/shard_map/ppermute | solution.py:303
  13.9 10.4 %shard_map.28 = (f32[256,256]{1,0:T(8,128)S(1)}, bf16[128,1408]{1,0:T(8,128)(2,1)S(1)}) custom-call(s32[2]{0:T(128)S(1)} %pad_add_fusion.at_ref, bf16[128,1024]{1,0:T(8,128)(2,1)S(1)} %bitcast.10, bf16[128,1024]{1,0:T(8,128)(2,1)S(1)} %collective-permute-done.other_ref, f32[1,2048]{1,0:T(1,128)S(1)} %copy-done.1), custom_call_target="tpu_custom_call" | custom-call | flops 20000000000 | bytes 1048576 | tf_op jit(solution)/shard_map/pallas_call | solution.py:163
  24.3 8.3 %collective-permute-done.3.refs_1_ = bf16[2,128,1024]{2,1,0:T(8,128)(2,1)S(1)} collective-permute-done((bf16[2,128,1024]{2,1,0:T(8,128)(2,1)S(1)}, bf16[2,128,1024]{2,1,0:T(8,128)(2,1)S(1)}, u32[]{:S(2)}, u32[]{:S(2)}) %collective-permute-start.3) | collective-permute-done | bytes 524320 | tf_op jit(solution)/shard_map/ppermute | solution.py:303
  32.6 2.3 %collective-permute-start.8 = (bf16[128,1024]{1,0:T(8,128)(2,1)S(1)}, bf16[128,1024]{1,0:T(8,128)(2,1)S(1)}, u32[]{:S(2)}, u32[]{:S(2)}) collective-permute-start(bf16[128,1024]{1,0:T(8,128)(2,1)S(1)} %collective-permute-done.1), channel_id=1, source_target_pairs={{0,16},{1,17},{2,18},{3,19},{4,20},{5,21},{6,22},{7,23},{8,24},{9,... | collective-permute-start | bytes 786440 | tf_op jit(solution)/shard_map/ppermute | solution.py:303
  36.2 2.0 %collective-permute-start.6 = (bf16[128,1408]{1,0:T(8,128)(2,1)S(1)}, bf16[128,1408]{1,0:T(8,128)(2,1)S(1)}, u32[]{:S(2)}, u32[]{:S(2)}) collective-permute-start(bf16[128,1408]{1,0:T(8,128)(2,1)S(1)} %get-tuple-element.24), channel_id=1, source_target_pairs={{0,6},{1,97}} | collective-permute-start | bytes 1081352 | tf_op jit(solution)/shard_map/ppermute | solution.py:303
  38.3 1.3 %collective-permute-start.5 = (bf16[128,1408]{1,0:T(8,128)(2,1)S(1)}, bf16[128,1408]{1,0:T(8,128)(2,1)S(1)}, u32[]{:S(2)}, u32[]{:S(2)}) collective-permute-start(bf16[128,1408]{1,0:T(8,128)(2,1)S(1)} %get-tuple-element.24), channel_id=1, source_target_pairs={{0,2},{1,33}} | collective-permute-start | bytes 1081352 | tf_op jit(solution)/shard_map/ppermute | solution.py:303
  39.6 2.6 %collective-permute-done.8 = bf16[128,1024]{1,0:T(8,128)(2,1)S(1)} collective-permute-done((bf16[128,1024]{1,0:T(8,128)(2,1)S(1)}, bf16[128,1024]{1,0:T(8,128)(2,1)S(1)}, u32[]{:S(2)}, u32[]{:S(2)}) %collective-permute-start.8) | collective-permute-done | bytes 262176 | tf_op jit(solution)/shard_map/ppermute | solution.py:303
  42.6 1.8 %collective-permute-done.5 = bf16[128,1408]{1,0:T(8,128)(2,1)S(1)} collective-permute-done((bf16[128,1408]{1,0:T(8,128)(2,1)S(1)}, bf16[128,1408]{1,0:T(8,128)(2,1)S(1)}, u32[]{:S(2)}, u32[]{:S(2)}) %collective-permute-start.5) | collective-permute-done | bytes 360480 | tf_op jit(solution)/shard_map/ppermute | solution.py:303
  44.5 2.0 %collective-permute-start.11 = (bf16[128,1408]{1,0:T(8,128)(2,1)S(1)}, bf16[128,1408]{1,0:T(8,128)(2,1)S(1)}, u32[]{:S(2)}, u32[]{:S(2)}) collective-permute-start(bf16[128,1408]{1,0:T(8,128)(2,1)S(1)} %add_add_fusion.2), channel_id=1, source_target_pairs={{0,64},{2,66},{6,70},{4,68},{1,17},{33,49},{97,113},{65,81}} | collective-permute-start | bytes 1081352 | tf_op jit(solution)/shard_map/ppermute | solution.py:303
  46.5 1.3 %collective-permute-start.10 = (bf16[128,1408]{1,0:T(8,128)(2,1)S(1)}, bf16[128,1408]{1,0:T(8,128)(2,1)S(1)}, u32[]{:S(2)}, u32[]{:S(2)}) collective-permute-start(bf16[128,1408]{1,0:T(8,128)(2,1)S(1)} %add_add_fusion.2), channel_id=1, source_target_pairs={{0,96},{2,98},{6,102},{4,100},{1,25},{33,57},{97,121},{65,89}} | collective-permute-start | bytes 1081352 | tf_op jit(solution)/shard_map/ppermute | solution.py:303
  47.8 1.3 %collective-permute-start.9 = (bf16[128,1408]{1,0:T(8,128)(2,1)S(1)}, bf16[128,1408]{1,0:T(8,128)(2,1)S(1)}, u32[]{:S(2)}, u32[]{:S(2)}) collective-permute-start(bf16[128,1408]{1,0:T(8,128)(2,1)S(1)} %add_add_fusion.2), channel_id=1, source_target_pairs={{0,32},{2,34},{6,38},{4,36},{1,9},{33,41},{97,105},{65,73}} | collective-permute-start | bytes 1081352 | tf_op jit(solution)/shard_map/ppermute | solution.py:303
  49.4 1.5 %collective-permute-done.11 = bf16[128,1408]{1,0:T(8,128)(2,1)S(1)} collective-permute-done((bf16[128,1408]{1,0:T(8,128)(2,1)S(1)}, bf16[128,1408]{1,0:T(8,128)(2,1)S(1)}, u32[]{:S(2)}, u32[]{:S(2)}) %collective-permute-start.11) | collective-permute-done | bytes 360480 | tf_op jit(solution)/shard_map/ppermute | solution.py:303
  50.9 2.1 %collective-permute-start.21 = (bf16[2,128,1024]{2,1,0:T(8,128)(2,1)S(1)}, bf16[2,128,1024]{2,1,0:T(8,128)(2,1)S(1)}, u32[]{:S(2)}, u32[]{:S(2)}) collective-permute-start(bf16[2,128,1024]{2,1,0:T(8,128)(2,1)S(1)} %pad_maximum_fusion.1.refs_8_), channel_id=1, source_target_pairs={{0,96},{1,97},{2,98},{3,99},{4,100},{5,101},{6,102},{7,103},{8,104... | collective-permute-start | bytes 1572872 | tf_op jit(solution)/shard_map/ppermute | solution.py:303
  52.9 1.8 %collective-permute-done.9 = bf16[128,1408]{1,0:T(8,128)(2,1)S(1)} collective-permute-done((bf16[128,1408]{1,0:T(8,128)(2,1)S(1)}, bf16[128,1408]{1,0:T(8,128)(2,1)S(1)}, u32[]{:S(2)}, u32[]{:S(2)}) %collective-permute-start.9) | collective-permute-done | bytes 360480 | tf_op jit(solution)/shard_map/ppermute | solution.py:303
  54.8 9.5 %collective-permute-done.12.refs_3_ = bf16[2,128,1024]{2,1,0:T(8,128)(2,1)S(1)} collective-permute-done((bf16[2,128,1024]{2,1,0:T(8,128)(2,1)S(1)}, bf16[2,128,1024]{2,1,0:T(8,128)(2,1)S(1)}, u32[]{:S(2)}, u32[]{:S(2)}) %collective-permute-start.12) | collective-permute-done | bytes 524320 | tf_op jit(solution)/shard_map/ppermute | solution.py:303
  65.6 1.3 %collective-permute-start.18 = (bf16[128,1408]{1,0:T(8,128)(2,1)S(1)}, bf16[128,1408]{1,0:T(8,128)(2,1)S(1)}, u32[]{:S(2)}, u32[]{:S(2)}) collective-permute-start(bf16[128,1408]{1,0:T(8,128)(2,1)S(1)} %add_add_fusion.1), channel_id=1, source_target_pairs={{0,24},{2,26},{6,30},{4,28},{32,56},{34,58},{38,62},{36,60},{96,12... | collective-permute-start | bytes 1081352 | tf_op jit(solution)/shard_map/ppermute | solution.py:303
  68.4 3.1 %collective-permute-done.21.refs_10_ = bf16[2,128,1024]{2,1,0:T(8,128)(2,1)S(1)} collective-permute-done((bf16[2,128,1024]{2,1,0:T(8,128)(2,1)S(1)}, bf16[2,128,1024]{2,1,0:T(8,128)(2,1)S(1)}, u32[]{:S(2)}, u32[]{:S(2)}) %collective-permute-start.21) | collective-permute-done | bytes 524320 | tf_op jit(solution)/shard_map/ppermute | solution.py:303
  71.5 3.5 %collective-permute-start.13 = (bf16[2,128,1024]{2,1,0:T(8,128)(2,1)S(1)}, bf16[2,128,1024]{2,1,0:T(8,128)(2,1)S(1)}, u32[]{:S(2)}, u32[]{:S(2)}) collective-permute-start(bf16[2,128,1024]{2,1,0:T(8,128)(2,1)S(1)} %pad_maximum_fusion.refs_0_), channel_id=1, source_target_pairs={{0,1},{1,0},{2,3},{3,2},{4,5},{5,4},{6,7},{7,6},{8,9},{9,8},{10,11... | collective-permute-start | bytes 1572872 | tf_op jit(solution)/shard_map/ppermute | solution.py:303
  75.5 2.2 %collective-permute-start.16 = (bf16[2,128,1024]{2,1,0:T(8,128)(2,1)S(1)}, bf16[2,128,1024]{2,1,0:T(8,128)(2,1)S(1)}, u32[]{:S(2)}, u32[]{:S(2)}) collective-permute-start(bf16[2,128,1024]{2,1,0:T(8,128)(2,1)S(1)} %collective-permute-done.12.refs_3_), channel_id=1, source_target_pairs={{0,1},{1,0},{2,3},{3,2},{4,5},{5,4},{6,7},{7,6},{8,9},{9,8},{10,11... | collective-permute-start | bytes 1572872 | tf_op jit(solution)/shard_map/ppermute | solution.py:303
  77.8 1.3 %collective-permute-done.20.refs_9_ = bf16[2,128,1024]{2,1,0:T(8,128)(2,1)S(1)} collective-permute-done((bf16[2,128,1024]{2,1,0:T(8,128)(2,1)S(1)}, bf16[2,128,1024]{2,1,0:T(8,128)(2,1)S(1)}, u32[]{:S(2)}, u32[]{:S(2)}) %collective-permute-start.20) | collective-permute-done | bytes 524320 | tf_op jit(solution)/shard_map/ppermute | solution.py:303
  79.2 4.7 %collective-permute-start.23 = (bf16[128,1408]{1,0:T(8,128)(2,1)S(1)}, bf16[128,1408]{1,0:T(8,128)(2,1)S(1)}, u32[]{:S(2)}, u32[]{:S(2)}) collective-permute-start(bf16[128,1408]{1,0:T(8,128)(2,1)S(1)} %add_add_fusion.refs_12_), channel_id=1, source_target_pairs={{0,1},{1,0},{2,3},{3,2},{4,5},{5,4},{6,7},{7,6},{8,9},{9,8},{10,11... | collective-permute-start | bytes 1081352 | tf_op jit(solution)/shard_map/ppermute | solution.py:303
  85.2 19.0 %shard_map.29 = f32[2048,8,128]{2,1,0:T(8,128)} custom-call(s32[2]{0:T(128)S(1)} %pad_add_fusion.at_ref, bf16[2,128,1024]{2,1,0:T(8,128)(2,1)S(1)} %pad_maximum_fusion.refs_0_, bf16[2,128,1024]{2,1,0:T(8,128)(2,1)S(1)} %collective-permute-done.3.refs_1_, bf16[2,128,1024]{2,1,0:T(8,128)(2,1)S(1)} %collective-permute-done.4.refs_2_, ...), custom_call_target="tpu_custom_call" | custom-call | tf_op jit(solution)/shard_map/pallas_call | solution.py:273
  (44 shorter events, 11.4 us)
Async XLA Ops:
  0.0 9.6 %collective-permute-start.2 = (bf16[128,1024]{1,0:T(8,128)(2,1)}, bf16[128,1024]{1,0:T(8,128)(2,1)S(1)}, u32[]{:S(2)}, u32[]{:S(2)}) collective-permute-start(bf16[128,1024]{1,0:T(8,128)(2,1)} %bitcast.7), channel_id=1, source_target_pairs={{0,8},{1,9},{2,10},{3,11},{4,12},{5,13},{6,14},{7,15},{8,0},{9,1},... | collective-permute-start | bytes 786440 | tf_op jit(solution)/shard_map/ppermute | solution.py:303
  2.5 9.7 %collective-permute-start = (bf16[128,1024]{1,0:T(8,128)(2,1)}, bf16[128,1024]{1,0:T(8,128)(2,1)S(1)}, u32[]{:S(2)}, u32[]{:S(2)}) collective-permute-start(bf16[128,1024]{1,0:T(8,128)(2,1)} %bitcast.8), channel_id=1, source_target_pairs={{0,1},{1,0},{2,3},{3,2},{4,5},{5,4},{6,7},{7,6},{8,9},{9,8},{10,11... | collective-permute-start | bytes 786440 | tf_op jit(solution)/shard_map/ppermute | solution.py:303
  3.4 20.8 %collective-permute-start.1 = (bf16[128,1024]{1,0:T(8,128)(2,1)}, bf16[128,1024]{1,0:T(8,128)(2,1)S(1)}, u32[]{:S(2)}, u32[]{:S(2)}) collective-permute-start(bf16[128,1024]{1,0:T(8,128)(2,1)} %bitcast.9), channel_id=1, source_target_pairs={{0,0},{1,16},{2,8},{3,24},{4,32},{5,48},{6,40},{7,56},{8,64},{9,80... | collective-permute-start | bytes 786440 | tf_op jit(solution)/shard_map/ppermute | solution.py:303
  10.7 13.6 %collective-permute-start.4 = (bf16[2,128,1024]{2,1,0:T(8,128)(2,1)S(1)}, bf16[2,128,1024]{2,1,0:T(8,128)(2,1)S(1)}, u32[]{:S(2)}, u32[]{:S(2)}) collective-permute-start(bf16[2,128,1024]{2,1,0:T(8,128)(2,1)S(1)} %pad_maximum_fusion.refs_0_), channel_id=1, source_target_pairs={{0,6},{1,7},{2,0},{3,1},{4,2},{5,3},{6,4},{7,5},{8,14},{9,15},{10,... | collective-permute-start | bytes 1572872 | tf_op jit(solution)/shard_map/ppermute | solution.py:303
  12.1 20.5 %collective-permute-start.3 = (bf16[2,128,1024]{2,1,0:T(8,128)(2,1)S(1)}, bf16[2,128,1024]{2,1,0:T(8,128)(2,1)S(1)}, u32[]{:S(2)}, u32[]{:S(2)}) collective-permute-start(bf16[2,128,1024]{2,1,0:T(8,128)(2,1)S(1)} %pad_maximum_fusion.refs_0_), channel_id=1, source_target_pairs={{0,2},{1,3},{2,4},{3,5},{4,6},{5,7},{6,0},{7,1},{8,10},{9,11},{10,... | collective-permute-start | bytes 1572872 | tf_op jit(solution)/shard_map/ppermute | solution.py:303
  32.6 9.6 %collective-permute-start.8 = (bf16[128,1024]{1,0:T(8,128)(2,1)S(1)}, bf16[128,1024]{1,0:T(8,128)(2,1)S(1)}, u32[]{:S(2)}, u32[]{:S(2)}) collective-permute-start(bf16[128,1024]{1,0:T(8,128)(2,1)S(1)} %collective-permute-done.1), channel_id=1, source_target_pairs={{0,16},{1,17},{2,18},{3,19},{4,20},{5,21},{6,22},{7,23},{8,24},{9,... | collective-permute-start | bytes 786440 | tf_op jit(solution)/shard_map/ppermute | solution.py:303
  34.9 7.4 %collective-permute-start.7 = (bf16[128,1408]{1,0:T(8,128)(2,1)S(1)}, bf16[128,1408]{1,0:T(8,128)(2,1)S(1)}, u32[]{:S(2)}, u32[]{:S(2)}) collective-permute-start(bf16[128,1408]{1,0:T(8,128)(2,1)S(1)} %get-tuple-element.24), channel_id=1, source_target_pairs={{0,4},{1,65}} | collective-permute-start | bytes 1081352 | tf_op jit(solution)/shard_map/ppermute | solution.py:303
  36.2 6.4 %collective-permute-start.6 = (bf16[128,1408]{1,0:T(8,128)(2,1)S(1)}, bf16[128,1408]{1,0:T(8,128)(2,1)S(1)}, u32[]{:S(2)}, u32[]{:S(2)}) collective-permute-start(bf16[128,1408]{1,0:T(8,128)(2,1)S(1)} %get-tuple-element.24), channel_id=1, source_target_pairs={{0,6},{1,97}} | collective-permute-start | bytes 1081352 | tf_op jit(solution)/shard_map/ppermute | solution.py:303
  38.3 6.1 %collective-permute-start.5 = (bf16[128,1408]{1,0:T(8,128)(2,1)S(1)}, bf16[128,1408]{1,0:T(8,128)(2,1)S(1)}, u32[]{:S(2)}, u32[]{:S(2)}) collective-permute-start(bf16[128,1408]{1,0:T(8,128)(2,1)S(1)} %get-tuple-element.24), channel_id=1, source_target_pairs={{0,2},{1,33}} | collective-permute-start | bytes 1081352 | tf_op jit(solution)/shard_map/ppermute | solution.py:303
  44.5 6.4 %collective-permute-start.11 = (bf16[128,1408]{1,0:T(8,128)(2,1)S(1)}, bf16[128,1408]{1,0:T(8,128)(2,1)S(1)}, u32[]{:S(2)}, u32[]{:S(2)}) collective-permute-start(bf16[128,1408]{1,0:T(8,128)(2,1)S(1)} %add_add_fusion.2), channel_id=1, source_target_pairs={{0,64},{2,66},{6,70},{4,68},{1,17},{33,49},{97,113},{65,81}} | collective-permute-start | bytes 1081352 | tf_op jit(solution)/shard_map/ppermute | solution.py:303
  46.5 6.4 %collective-permute-start.10 = (bf16[128,1408]{1,0:T(8,128)(2,1)S(1)}, bf16[128,1408]{1,0:T(8,128)(2,1)S(1)}, u32[]{:S(2)}, u32[]{:S(2)}) collective-permute-start(bf16[128,1408]{1,0:T(8,128)(2,1)S(1)} %add_add_fusion.2), channel_id=1, source_target_pairs={{0,96},{2,98},{6,102},{4,100},{1,25},{33,57},{97,121},{65,89}} | collective-permute-start | bytes 1081352 | tf_op jit(solution)/shard_map/ppermute | solution.py:303
  47.8 6.9 %collective-permute-start.9 = (bf16[128,1408]{1,0:T(8,128)(2,1)S(1)}, bf16[128,1408]{1,0:T(8,128)(2,1)S(1)}, u32[]{:S(2)}, u32[]{:S(2)}) collective-permute-start(bf16[128,1408]{1,0:T(8,128)(2,1)S(1)} %add_add_fusion.2), channel_id=1, source_target_pairs={{0,32},{2,34},{6,38},{4,36},{1,9},{33,41},{97,105},{65,73}} | collective-permute-start | bytes 1081352 | tf_op jit(solution)/shard_map/ppermute | solution.py:303
  49.2 15.1 %collective-permute-start.12 = (bf16[2,128,1024]{2,1,0:T(8,128)(2,1)S(1)}, bf16[2,128,1024]{2,1,0:T(8,128)(2,1)S(1)}, u32[]{:S(2)}, u32[]{:S(2)}) collective-permute-start(bf16[2,128,1024]{2,1,0:T(8,128)(2,1)S(1)} %pad_maximum_fusion.refs_0_), channel_id=1, source_target_pairs={{0,4},{1,5},{2,6},{3,7},{4,0},{5,1},{6,2},{7,3},{8,12},{9,13},{10,... | collective-permute-start | bytes 1572872 | tf_op jit(solution)/shard_map/ppermute | solution.py:303
  49.3 19.0 %collective-permute-start.22 = (bf16[2,128,1024]{2,1,0:T(8,128)(2,1)S(1)}, bf16[2,128,1024]{2,1,0:T(8,128)(2,1)S(1)}, u32[]{:S(2)}, u32[]{:S(2)}) collective-permute-start(bf16[2,128,1024]{2,1,0:T(8,128)(2,1)S(1)} %pad_maximum_fusion.1.refs_8_), channel_id=1, source_target_pairs={{0,64},{1,65},{2,66},{3,67},{4,68},{5,69},{6,70},{7,71},{8,72},{9,... | collective-permute-start | bytes 1572872 | tf_op jit(solution)/shard_map/ppermute | solution.py:303
  50.9 20.7 %collective-permute-start.21 = (bf16[2,128,1024]{2,1,0:T(8,128)(2,1)S(1)}, bf16[2,128,1024]{2,1,0:T(8,128)(2,1)S(1)}, u32[]{:S(2)}, u32[]{:S(2)}) collective-permute-start(bf16[2,128,1024]{2,1,0:T(8,128)(2,1)S(1)} %pad_maximum_fusion.1.refs_8_), channel_id=1, source_target_pairs={{0,96},{1,97},{2,98},{3,99},{4,100},{5,101},{6,102},{7,103},{8,104... | collective-permute-start | bytes 1572872 | tf_op jit(solution)/shard_map/ppermute | solution.py:303
  64.3 10.7 %collective-permute-start.19 = (bf16[128,1408]{1,0:T(8,128)(2,1)S(1)}, bf16[128,1408]{1,0:T(8,128)(2,1)S(1)}, u32[]{:S(2)}, u32[]{:S(2)}) collective-permute-start(bf16[128,1408]{1,0:T(8,128)(2,1)S(1)} %add_add_fusion.1), channel_id=1, source_target_pairs={{0,16},{2,18},{6,22},{4,20},{32,48},{34,50},{38,54},{36,52},{96,11... | collective-permute-start | bytes 1081352 | tf_op jit(solution)/shard_map/ppermute | solution.py:303
  65.6 9.5 %collective-permute-start.18 = (bf16[128,1408]{1,0:T(8,128)(2,1)S(1)}, bf16[128,1408]{1,0:T(8,128)(2,1)S(1)}, u32[]{:S(2)}, u32[]{:S(2)}) collective-permute-start(bf16[128,1408]{1,0:T(8,128)(2,1)S(1)} %add_add_fusion.1), channel_id=1, source_target_pairs={{0,24},{2,26},{6,30},{4,28},{32,56},{34,58},{38,62},{36,60},{96,12... | collective-permute-start | bytes 1081352 | tf_op jit(solution)/shard_map/ppermute | solution.py:303
  66.9 8.6 %collective-permute-start.17 = (bf16[128,1408]{1,0:T(8,128)(2,1)S(1)}, bf16[128,1408]{1,0:T(8,128)(2,1)S(1)}, u32[]{:S(2)}, u32[]{:S(2)}) collective-permute-start(bf16[128,1408]{1,0:T(8,128)(2,1)S(1)} %add_add_fusion.1), channel_id=1, source_target_pairs={{0,8},{2,10},{6,14},{4,12},{32,40},{34,42},{38,46},{36,44},{96,104... | collective-permute-start | bytes 1081352 | tf_op jit(solution)/shard_map/ppermute | solution.py:303
  68.3 10.9 %collective-permute-start.20 = (bf16[2,128,1024]{2,1,0:T(8,128)(2,1)S(1)}, bf16[2,128,1024]{2,1,0:T(8,128)(2,1)S(1)}, u32[]{:S(2)}, u32[]{:S(2)}) collective-permute-start(bf16[2,128,1024]{2,1,0:T(8,128)(2,1)S(1)} %pad_maximum_fusion.1.refs_8_), channel_id=1, source_target_pairs={{0,32},{1,33},{2,34},{3,35},{4,36},{5,37},{6,38},{7,39},{8,40},{9,... | collective-permute-start | bytes 1572872 | tf_op jit(solution)/shard_map/ppermute | solution.py:303
  71.5 12.4 %collective-permute-start.13 = (bf16[2,128,1024]{2,1,0:T(8,128)(2,1)S(1)}, bf16[2,128,1024]{2,1,0:T(8,128)(2,1)S(1)}, u32[]{:S(2)}, u32[]{:S(2)}) collective-permute-start(bf16[2,128,1024]{2,1,0:T(8,128)(2,1)S(1)} %pad_maximum_fusion.refs_0_), channel_id=1, source_target_pairs={{0,1},{1,0},{2,3},{3,2},{4,5},{5,4},{6,7},{7,6},{8,9},{9,8},{10,11... | collective-permute-start | bytes 1572872 | tf_op jit(solution)/shard_map/ppermute | solution.py:303
  75.0 8.9 %collective-permute-start.14 = (bf16[2,128,1024]{2,1,0:T(8,128)(2,1)S(1)}, bf16[2,128,1024]{2,1,0:T(8,128)(2,1)S(1)}, u32[]{:S(2)}, u32[]{:S(2)}) collective-permute-start(bf16[2,128,1024]{2,1,0:T(8,128)(2,1)S(1)} %collective-permute-done.3.refs_1_), channel_id=1, source_target_pairs={{0,1},{1,0},{2,3},{3,2},{4,5},{5,4},{6,7},{7,6},{8,9},{9,8},{10,11... | collective-permute-start | bytes 1572872 | tf_op jit(solution)/shard_map/ppermute | solution.py:303
  75.1 8.8 %collective-permute-start.15 = (bf16[2,128,1024]{2,1,0:T(8,128)(2,1)S(1)}, bf16[2,128,1024]{2,1,0:T(8,128)(2,1)S(1)}, u32[]{:S(2)}, u32[]{:S(2)}) collective-permute-start(bf16[2,128,1024]{2,1,0:T(8,128)(2,1)S(1)} %collective-permute-done.4.refs_2_), channel_id=1, source_target_pairs={{0,1},{1,0},{2,3},{3,2},{4,5},{5,4},{6,7},{7,6},{8,9},{9,8},{10,11... | collective-permute-start | bytes 1572872 | tf_op jit(solution)/shard_map/ppermute | solution.py:303
  75.5 8.4 %collective-permute-start.16 = (bf16[2,128,1024]{2,1,0:T(8,128)(2,1)S(1)}, bf16[2,128,1024]{2,1,0:T(8,128)(2,1)S(1)}, u32[]{:S(2)}, u32[]{:S(2)}) collective-permute-start(bf16[2,128,1024]{2,1,0:T(8,128)(2,1)S(1)} %collective-permute-done.12.refs_3_), channel_id=1, source_target_pairs={{0,1},{1,0},{2,3},{3,2},{4,5},{5,4},{6,7},{7,6},{8,9},{9,8},{10,11... | collective-permute-start | bytes 1572872 | tf_op jit(solution)/shard_map/ppermute | solution.py:303
  79.2 6.0 %collective-permute-start.23 = (bf16[128,1408]{1,0:T(8,128)(2,1)S(1)}, bf16[128,1408]{1,0:T(8,128)(2,1)S(1)}, u32[]{:S(2)}, u32[]{:S(2)}) collective-permute-start(bf16[128,1408]{1,0:T(8,128)(2,1)S(1)} %add_add_fusion.refs_12_), channel_id=1, source_target_pairs={{0,1},{1,0},{2,3},{3,2},{4,5},{5,4},{6,7},{7,6},{8,9},{9,8},{10,11... | collective-permute-start | bytes 1081352 | tf_op jit(solution)/shard_map/ppermute | solution.py:303
  (6 other events, 113.9 us)

commit v4 on v3

--- a/solution.py
+++ b/solution.py
@@ -12,8 +12,8 @@
 TILES = 8
 NPCOL = 16
 MB = 512
+OFFSETS = (0, 1, 3, 2)
 MSG = R + 384
-STEPS = TILES * NB // MB
 f32 = jnp.float32
 bf16 = jnp.bfloat16
 HIGHEST = lax.Precision.HIGHEST
@@ -77,7 +77,7 @@
 
 def spread_rounds():
     held = {0: [(0, 0, 0, 0, 0)], 1: [(0, 0, 0, 0, 1)]}
-    order = {0: "xyz", 1: "yzx"}
+    order = {0: "yzx", 1: "zxy"}
     rounds = []
     for step in range(3):
         ops = []
@@ -171,125 +171,145 @@
     )(at, own, other, shift)
 
 
+def rows_of(mine, theirs, n):
+    return jnp.concatenate([mine[n][0], theirs[n][0], mine[n][1], theirs[n][1]], 0)
+
+
+def base_kernel(*refs):
+    mine, theirs, cols_ref, out_ref = refs[0:4], refs[4:8], refs[8], refs[9]
+    cols = jnp.concatenate([cols_ref[0], cols_ref[1]], 0)
+    for n in range(4):
+        out_ref[n * MB:n * MB + MB, :] = dot(rows_of(mine, theirs, n), cols, NT)
+
+
+def base(mine, theirs, cols):
+    vm = pl.BlockSpec(memory_space=pltpu.VMEM)
+    return pl.pallas_call(
+        base_kernel,
+        out_shape=jax.ShapeDtypeStruct((TILES * NB, NB), f32),
+        in_specs=[vm] * 9,
+        out_specs=vm,
+        compiler_params=pltpu.CompilerParams(vmem_limit_bytes=16 << 20),
+        cost_estimate=pl.CostEstimate(flops=2 * TILES * NB * NB * R, bytes_accessed=8 << 20, transcendentals=0),
+    )(*mine, *theirs, cols)
+
+
 def tail_kernel(at_ref, *refs):
-    mine, theirs, cols = refs[0:4], refs[4:8], refs[8:12]
-    lead_ref, other_ref, shift_ref, chol_ref, out_ref, f, a, hhi, hlo, f0, w, ghi_ref, glo_ref, stage, sem = refs[12:]
+    mine, theirs, cols, bases = refs[0:4], refs[4:8], refs[8:12], refs[12:16]
+    lead_ref, other_ref, shift_ref, chol_ref, out_ref, f0, w, ghi_ref, glo_ref, lq, stage, sem = refs[16:]
     p, q = at_ref[0], at_ref[1]
     y, zh = p // 2, p % 2
     zl, x, core = q // 8, q // 2 % 4, q % 2
-    g = pl.program_id(0)
-
-    def shard(n):
-        return pl.ds(pl.multiple_of(n * SHARD, SHARD), SHARD)
-
-    @pl.when(g == 0)
-    def _():
-        for n, d in enumerate((0, 1, 3, 2)):
-            for j in range(2):
-                for bufs, whose in ((mine, core), (theirs, 1 - core)):
-                    tile = (zl + j) % 2 * 4 + (x + 4 - d) % 4
-                    f[shard(tile * 2 + whose), :] = bufs[n][j]
-                a[shard((y + 4 - d) % 4 * 2 + (zh + j) % 2), :] = cols[n][j]
-        f0[pl.ds(pl.multiple_of(core * SHARD, SHARD), SHARD), :] = lead_ref[:, :R]
-        f0[pl.ds(pl.multiple_of((1 - core) * SHARD, SHARD), SHARD), :] = other_ref[:, :R]
-        for n, (own, other) in enumerate(((lead_ref, other_ref), (other_ref, lead_ref))):
-            part = jnp.where(core == 0, own[:, R:], other[:, R:])
-            w[n, :128, :128] = part[:, :128]
-            w[n, :128, 128:] = jnp.zeros((128, 128), bf16)
-            w[n, 128:, :] = part[:, 128:]
-        ghi, glo = split(dot(w[0], f0[...], NN) + dot(w[1], f0[...], NN))
-        ghi_ref[...] = ghi
-        glo_ref[...] = glo
-        lhi, llo = split(dot(a[...], ghi_ref[...], NT) + dot(a[...], glo_ref[...], NT))
-        for k in range(4):
-            at = pl.ds(k * NB, NB)
-            h = a[:, at].astype(f32) - (
-                dot(lhi, ghi_ref[:, at], NN) + dot(lhi, glo_ref[:, at], NN) + dot(llo, ghi_ref[:, at], NN)
-            )
-            hi, lo = split(h)
-            hhi[:, at] = hi
-            hlo[:, at] = lo
-
-        @pl.when(q == 0)
-        def _():
-            hhi[pl.ds(0, NB), :] = ghi_ref[...]
-            hlo[pl.ds(0, NB), :] = glo_ref[...]
-
-    def puts(step, slot):
+
+    f0[pl.ds(pl.multiple_of(core * SHARD, SHARD), SHARD), :] = lead_ref[:, :R]
+    f0[pl.ds(pl.multiple_of((1 - core) * SHARD, SHARD), SHARD), :] = other_ref[:, :R]
+    for n, (own, other) in enumerate(((lead_ref, other_ref), (other_ref, lead_ref))):
+        part = jnp.where(core == 0, own[:, R:], other[:, R:])
+        w[n, :128, :128] = part[:, :128]
+        w[n, :128, 128:] = jnp.zeros((128, 128), bf16)
+        w[n, 128:, :] = part[:, 128:]
+    ghi, glo = split(dot(w[0], f0[...], NN) + dot(w[1], f0[...], NN))
+    ghi_ref[...] = ghi
+    glo_ref[...] = glo
+
+    def panel(factor_rows):
+        return dot(factor_rows, ghi_ref[...], NT) + dot(factor_rows, glo_ref[...], NT)
+
+    for m in range(4):
+        hi, lo = split(panel(jnp.concatenate([cols[m][0], cols[m][1]], 0)))
+        lq[m] = jnp.concatenate([hi, lo, hi], 1)
+
+    row = lax.broadcasted_iota(jnp.int32, (NB, NB), 0)
+    col = lax.broadcasted_iota(jnp.int32, (NB, NB), 1)
+    tile = [[(zl + j) % 2 * 4 + (x + 4 - d) % 4 for j in range(2)] for d in OFFSETS]
+
+    def puts(n):
         return [
             pltpu.make_async_copy(
-                stage.at[slot, :, pl.ds(c * 128, 128)],
-                out_ref.at[pl.ds(pl.multiple_of(step * MB, MB), MB), c, :],
-                sem.at[slot, c],
+                stage.at[n % 2, pl.ds(j * NB, NB), pl.ds(c * 128, 128)],
+                out_ref.at[pl.ds(pl.multiple_of(tile[n][j] * NB, NB), NB), c, :],
+                sem.at[n % 2, j, c],
             )
+            for j in range(2)
             for c in range(8)
         ]
 
-    slot = g % 2
-
-    @pl.when(g >= 2)
-    def _():
-        for copy in puts(g - 2, slot):
+    def place(n, j, own):
+        whose = core if own == 0 else 1 - core
+        return n % 2, pl.ds(pl.multiple_of(j * NB + whose * SHARD, SHARD), SHARD)
+
+    for n in range(4):
+        l = panel(rows_of(mine, theirs, n))
+        hi, lo = split(l)
+        lcat = jnp.concatenate([hi, hi, lo], 1)
+        if n >= 2:
+            for copy in puts(n - 2):
+                copy.wait()
+
+        def store(value, m, j, own):
+            slot, at = place(n, j, own)
+            k = (2 * j + own) * SHARD
+            for h in range(2):
+                c = (y + 4 - OFFSETS[m]) % 4 * 2 + (zh + h) % 2
+                cat = pl.ds(pl.multiple_of(c * 128, 128), 128)
+                stage[slot, at, cat] = value[k:k + SHARD, h * 128:h * 128 + 128]
+
+        for m in range(4):
+            value = bases[m][n * MB:n * MB + MB, :] - dot(lcat, lq[m], NT)
+            for j in range(2):
+                for own in range(2):
+                    store(value, m, j, own)
+        for j in range(2):
+            r = tile[n][j]
+            at = pl.ds(j * NB, NB)
+
+            @pl.when(q == 0)
+            def _():
+                for own in range(2):
+                    slot, rows = place(n, j, own)
+                    k = (2 * j + own) * SHARD
+                    stage[slot, rows, :NB] = l[k:k + SHARD, :]
+
+            @pl.when((p == 0) & (r == 0))
+            def _():
+                for m in range(4):
+                    for own in range(2):
+                        store(bases[m][n * MB:n * MB + MB, :], m, j, own)
+
+            @pl.when((p == q % 8) & (r % 2 == q // 8))
+            def _():
+                c = pl.ds(pl.multiple_of(r // 2 * NB, NB), NB)
+                stage[n % 2, at, c] += jnp.where(row == col, shift_ref[:, pl.ds(pl.multiple_of(r * NB, NB), NB)], 0.0)
+
+            @pl.when((p == 0) & (q == 0) & (r == 0))
+            def _():
+                stage[n % 2, at, :NB] = chol_ref[...].T
+
+        for copy in puts(n):
+            copy.start()
+    for n in range(2, 4):
+        for copy in puts(n):
             copy.wait()
 
-    ft = f[pl.ds(pl.multiple_of(g * MB, MB), MB), :]
-    for c in range(4):
-        at = pl.ds(c * NB, NB)
-        stage[slot, :, at] = dot(ft, hhi[at, :], NT) + dot(ft, hlo[at, :], NT)
-
-    @pl.when((g == 0) & (p == 0))
-    def _():
-        for c in range(4):
-            at = pl.ds(c * NB, NB)
-            stage[0, :NB, at] = dot(f[:NB, :], a[at, :], NT)
-
-    row = lax.broadcasted_iota(jnp.int32, (NB, NB), 0)
-    col = lax.broadcasted_iota(jnp.int32, (NB, NB), 1)
-    for t in range(MB // NB):
-        r = g * (MB // NB) + t
-        for c in range(4):
-            @pl.when((p == q % 8) & (r == 2 * c + q // 8))
-            def _():
-                shift = shift_ref[:, pl.ds(pl.multiple_of(r * NB, NB), NB)]
-                stage[slot, t * NB:t * NB + NB, c * NB:c * NB + NB] += jnp.where(row == col, shift, 0.0)
-
-    @pl.when((g == 0) & (p == 0) & (q == 0))
-    def _():
-        stage[0, :NB, :NB] = chol_ref[...].T
-
-    for copy in puts(g, slot):
-        copy.start()
-
-    @pl.when(g == STEPS - 1)
-    def _():
-        for copy in puts(g - 1, 1 - slot):
-            copy.wait()
-        for copy in puts(g, slot):
-            copy.wait()
-
-
-def tail(at, mine, theirs, cols, lead, other, shift, chol):
+
+def tail(at, mine, theirs, cols, bases, lead, other, shift, chol):
     vm = pl.BlockSpec(memory_space=pltpu.VMEM)
     return pl.pallas_call(
         tail_kernel,
-        grid=(STEPS,),
         out_shape=jax.ShapeDtypeStruct((TILES * NB, 8, 128), f32),
-        in_specs=[pl.BlockSpec(memory_space=pltpu.SMEM)] + [vm] * 16,
+        in_specs=[pl.BlockSpec(memory_space=pltpu.SMEM)] + [vm] * 20,
         out_specs=pl.BlockSpec(memory_space=pl.ANY),
         scratch_shapes=[
-            pltpu.VMEM((TILES * NB, R), bf16),
-            pltpu.VMEM((4 * NB, R), bf16),
-            pltpu.VMEM((4 * NB, R), bf16),
-            pltpu.VMEM((4 * NB, R), bf16),
             pltpu.VMEM((NB, R), bf16),
             pltpu.VMEM((2, NB, NB), bf16),
             pltpu.VMEM((NB, R), bf16),
             pltpu.VMEM((NB, R), bf16),
+            pltpu.VMEM((4, NB, 3 * NB), bf16),
             pltpu.VMEM((2, MB, 4 * NB), f32),
-            pltpu.SemaphoreType.DMA((2, 8)),
+            pltpu.SemaphoreType.DMA((2, 2, 8)),
         ],
-        compiler_params=pltpu.CompilerParams(vmem_limit_bytes=48 << 20),
-    )(at, *mine, *theirs, *cols, lead, other, shift, chol)
+        compiler_params=pltpu.CompilerParams(vmem_limit_bytes=24 << 20),
+    )(at, *mine, *theirs, *cols, *bases, lead, other, shift, chol)
 
 
 def local(factors, shift):
@@ -313,7 +333,7 @@
         return lead + (a + b + c)
 
     def star(piece, axis):
-        return [piece] + [send(piece, moves(lambda at: hop(at, axis, d))) for d in (1, 3, 2)]
+        return [piece] + [send(piece, moves(lambda at: hop(at, axis, d))) for d in OFFSETS[1:]]
 
     rounds = spread_rounds()
     chol, lead = factor(at, own, send(own, to_core), shift)
@@ -323,11 +343,13 @@
     pair = jnp.stack([piece, send(piece, moves(swap_zh))])
     lead, pair = lax.optimization_barrier((spread(lead, rounds[0]), pair))
     cols = star(pair, "y")
-    lead = spread(lead, rounds[1])
-    lead, *mine = lax.optimization_barrier((lead, *mine))
+    lead = after(spread(lead, rounds[1]), mine[3], *cols[1:])
     theirs = [send(value, to_core) for value in mine]
-    lead, *cols = lax.optimization_barrier((spread(lead, rounds[2]), *cols))
-    out = tail(at, mine, theirs, cols, lead, send(lead, to_core), shift, chol)
+    bases = [base(mine, theirs, value) for value in cols]
+    a, b, c = [send(lead, to) for to in rounds[2]]
+    lead = after(lead, *bases) + (a + b + c)
+    other = send(lead, to_core)
+    out = tail(at, mine, theirs, cols, bases, lead, other, shift, chol)
     return out.reshape(1, TILES * NB, 1, 4 * NB)
 
 

time: 105 us -> 101 us (0.962)
  starting transfers between devices: 38.8 us -> 32.1 us
  waiting for transfers between devices: 32.7 us -> 34.2 us
    ppermute x24, starting transfers between devices: 38.8 us -> 32.1 us  [send(): return lax.ppermute(value, both, pairs)]
    ppermute x24, waiting for transfers between devices: 32.7 us -> 34.2 us  [send(): return lax.ppermute(value, both, pairs)]
    pallas_call x1 -> x5, Pallas kernels: 19 us -> 20 us  [the longest x1 14.8 us: tail(): pl.pallas_call(tail_kernel, out_shape=jax.ShapeDtypeStruct((TILES * NB, 8...]
  transfers between devices with their start and end apart: 24 -> 24, of which waited for: 11 -> 12; matrix products, arithmetic and copies ran while one was open for 1% -> 1% of each run, Pallas kernels for 10% -> 16%
where the time goes in v4:
time: 101 us; the launch traced here: 100 us
  waiting for transfers between devices  34.2 us (34%)
  starting transfers between devices  32.1 us (32%)
  Pallas kernels  30.4 us (30%)
  local copies, waits for them, and re-layouts  1.65 us (2%)
  other arithmetic  1.36 us (1%)
    ppermute x24, waiting for transfers between devices, send(): return lax.ppermute(value, both, pairs)  34.2 us
    ppermute x24, starting transfers between devices, send(): return lax.ppermute(value, both, pairs)  32.1 us
    pallas_call x1, Pallas kernels, tail(): pl.pallas_call(tail_kernel, out_shape=jax.ShapeDtypeStruct((TILES * NB, 8...  14.8 us
    pallas_call x1, Pallas kernels, factor(): pl.pallas_call(factor_kernel, out_shape=[jax.ShapeDtypeStruct((NB, NB), f...  10.4 us
    pallas_call x4, Pallas kernels, base(): pl.pallas_call(base_kernel, out_shape=jax.ShapeDtypeStruct((TILES * NB, N...  5.15 us
  transfers between devices with their start and end apart: 24, of which 12 were waited for; matrix products, arithmetic and copies ran while one was open for 1% of the time, Pallas kernels for 16%

profile of v4, /device:TPU:1, one launch (start us, length us, event | category | flops | bytes accessed | tf_op | source)
XLA Modules:
  0.0 100.2 jit_solution(3945395349808356856)
XLA Ops:
  0.0 2.5 %collective-permute-start = (bf16[128,1024]{1,0:T(8,128)(2,1)}, bf16[128,1024]{1,0:T(8,128)(2,1)S(1)}, u32[]{:S(2)}, u32[]{:S(2)}) collective-permute-start(bf16[128,1024]{1,0:T(8,128)(2,1)} %bitcast.7), channel_id=1, source_target_pairs={{0,8},{1,9},{2,10},{3,11},{4,12},{5,13},{6,14},{7,15},{8,0},{9,1},... | collective-permute-start | bytes 786440 | tf_op jit(solution)/shard_map/ppermute | solution.py:323
  3.4 5.1 %collective-permute-start.2 = (bf16[128,1024]{1,0:T(8,128)(2,1)}, bf16[128,1024]{1,0:T(8,128)(2,1)S(1)}, u32[]{:S(2)}, u32[]{:S(2)}) collective-permute-start(bf16[128,1024]{1,0:T(8,128)(2,1)} %bitcast.9), channel_id=1, source_target_pairs={{0,0},{1,16},{2,8},{3,24},{4,32},{5,48},{6,40},{7,56},{8,64},{9,80... | collective-permute-start | bytes 786440 | tf_op jit(solution)/shard_map/ppermute | solution.py:323
  10.6 1.5 %collective-permute-start.4 = (bf16[2,128,1024]{2,1,0:T(8,128)(2,1)S(1)}, bf16[2,128,1024]{2,1,0:T(8,128)(2,1)S(1)}, u32[]{:S(2)}, u32[]{:S(2)}) collective-permute-start(bf16[2,128,1024]{2,1,0:T(8,128)(2,1)S(1)} %pad_maximum_fusion.refs_0_), channel_id=1, source_target_pairs={{0,6},{1,7},{2,0},{3,1},{4,2},{5,3},{6,4},{7,5},{8,14},{9,15},{10,... | collective-permute-start | bytes 1572872 | tf_op jit(solution)/shard_map/ppermute | solution.py:323
  13.8 10.4 %shard_map.28 = (f32[256,256]{1,0:T(8,128)S(1)}, bf16[128,1408]{1,0:T(8,128)(2,1)S(1)}) custom-call(s32[2]{0:T(128)S(1)} %pad_add_fusion.at_ref, bf16[128,1024]{1,0:T(8,128)(2,1)S(1)} %bitcast.10, bf16[128,1024]{1,0:T(8,128)(2,1)S(1)} %collective-permute-done.1.other_ref, f32[1,2048]{1,0:T(1,128)S(1)} %copy-done.1), custom_call_target="tpu_custom_call" | custom-call | flops 20000000000 | bytes 1048576 | tf_op jit(solution)/shard_map/pallas_call | solution.py:163
  24.3 8.4 %collective-permute-done.3.refs_1_ = bf16[2,128,1024]{2,1,0:T(8,128)(2,1)S(1)} collective-permute-done((bf16[2,128,1024]{2,1,0:T(8,128)(2,1)S(1)}, bf16[2,128,1024]{2,1,0:T(8,128)(2,1)S(1)}, u32[]{:S(2)}, u32[]{:S(2)}) %collective-permute-start.3) | collective-permute-done | bytes 524320 | tf_op jit(solution)/shard_map/ppermute | solution.py:323
  32.6 2.3 %collective-permute-start.13 = (bf16[128,1024]{1,0:T(8,128)(2,1)S(1)}, bf16[128,1024]{1,0:T(8,128)(2,1)S(1)}, u32[]{:S(2)}, u32[]{:S(2)}) collective-permute-start(bf16[128,1024]{1,0:T(8,128)(2,1)S(1)} %collective-permute-done.2), channel_id=1, source_target_pairs={{0,16},{1,17},{2,18},{3,19},{4,20},{5,21},{6,22},{7,23},{8,24},{9,... | collective-permute-start | bytes 786440 | tf_op jit(solution)/shard_map/ppermute | solution.py:323
  34.9 2.6 %collective-permute-start.12 = (bf16[128,1408]{1,0:T(8,128)(2,1)S(1)}, bf16[128,1408]{1,0:T(8,128)(2,1)S(1)}, u32[]{:S(2)}, u32[]{:S(2)}) collective-permute-start(bf16[128,1408]{1,0:T(8,128)(2,1)S(1)} %get-tuple-element.18), channel_id=1, source_target_pairs={{0,64},{1,17}} | collective-permute-start | bytes 1081352 | tf_op jit(solution)/shard_map/ppermute | solution.py:323
  37.5 1.8 %collective-permute-start.11 = (bf16[128,1408]{1,0:T(8,128)(2,1)S(1)}, bf16[128,1408]{1,0:T(8,128)(2,1)S(1)}, u32[]{:S(2)}, u32[]{:S(2)}) collective-permute-start(bf16[128,1408]{1,0:T(8,128)(2,1)S(1)} %get-tuple-element.18), channel_id=1, source_target_pairs={{0,96},{1,25}} | collective-permute-start | bytes 1081352 | tf_op jit(solution)/shard_map/ppermute | solution.py:323
  39.4 1.3 %collective-permute-start.10 = (bf16[128,1408]{1,0:T(8,128)(2,1)S(1)}, bf16[128,1408]{1,0:T(8,128)(2,1)S(1)}, u32[]{:S(2)}, u32[]{:S(2)}) collective-permute-start(bf16[128,1408]{1,0:T(8,128)(2,1)S(1)} %get-tuple-element.18), channel_id=1, source_target_pairs={{0,32},{1,9}} | collective-permute-start | bytes 1081352 | tf_op jit(solution)/shard_map/ppermute | solution.py:323
  40.8 1.5 %collective-permute-done.13 = bf16[128,1024]{1,0:T(8,128)(2,1)S(1)} collective-permute-done((bf16[128,1024]{1,0:T(8,128)(2,1)S(1)}, bf16[128,1024]{1,0:T(8,128)(2,1)S(1)}, u32[]{:S(2)}, u32[]{:S(2)}) %collective-permute-start.13) | collective-permute-done | bytes 262176 | tf_op jit(solution)/shard_map/ppermute | solution.py:323
  42.3 2.6 %collective-permute-done.12 = bf16[128,1408]{1,0:T(8,128)(2,1)S(1)} collective-permute-done((bf16[128,1408]{1,0:T(8,128)(2,1)S(1)}, bf16[128,1408]{1,0:T(8,128)(2,1)S(1)}, u32[]{:S(2)}, u32[]{:S(2)}) %collective-permute-start.12) | collective-permute-done | bytes 360480 | tf_op jit(solution)/shard_map/ppermute | solution.py:323
  44.9 1.7 %collective-permute-done.11 = bf16[128,1408]{1,0:T(8,128)(2,1)S(1)} collective-permute-done((bf16[128,1408]{1,0:T(8,128)(2,1)S(1)}, bf16[128,1408]{1,0:T(8,128)(2,1)S(1)}, u32[]{:S(2)}, u32[]{:S(2)}) %collective-permute-start.11) | collective-permute-done | bytes 360480 | tf_op jit(solution)/shard_map/ppermute | solution.py:323
  46.6 2.2 %collective-permute-done.10 = bf16[128,1408]{1,0:T(8,128)(2,1)S(1)} collective-permute-done((bf16[128,1408]{1,0:T(8,128)(2,1)S(1)}, bf16[128,1408]{1,0:T(8,128)(2,1)S(1)}, u32[]{:S(2)}, u32[]{:S(2)}) %collective-permute-start.10) | collective-permute-done | bytes 360480 | tf_op jit(solution)/shard_map/ppermute | solution.py:323
  49.0 1.3 %collective-permute-start.19 = (bf16[128,1408]{1,0:T(8,128)(2,1)S(1)}, bf16[128,1408]{1,0:T(8,128)(2,1)S(1)}, u32[]{:S(2)}, u32[]{:S(2)}) collective-permute-start(bf16[128,1408]{1,0:T(8,128)(2,1)S(1)} %add_add_fusion.2), channel_id=1, source_target_pairs={{0,16},{32,48},{96,112},{64,80},{1,5},{9,13},{25,29},{17,21}} | collective-permute-start | bytes 1081352 | tf_op jit(solution)/shard_map/ppermute | solution.py:323
  50.3 1.3 %collective-permute-start.18 = (bf16[128,1408]{1,0:T(8,128)(2,1)S(1)}, bf16[128,1408]{1,0:T(8,128)(2,1)S(1)}, u32[]{:S(2)}, u32[]{:S(2)}) collective-permute-start(bf16[128,1408]{1,0:T(8,128)(2,1)S(1)} %add_add_fusion.2), channel_id=1, source_target_pairs={{0,24},{32,56},{96,120},{64,88},{1,7},{9,15},{25,31},{17,23}} | collective-permute-start | bytes 1081352 | tf_op jit(solution)/shard_map/ppermute | solution.py:323
  51.7 4.2 %collective-permute-done.5.refs_3_ = bf16[2,128,1024]{2,1,0:T(8,128)(2,1)S(1)} collective-permute-done((bf16[2,128,1024]{2,1,0:T(8,128)(2,1)S(1)}, bf16[2,128,1024]{2,1,0:T(8,128)(2,1)S(1)}, u32[]{:S(2)}, u32[]{:S(2)}) %collective-permute-start.5) | collective-permute-done | bytes 524320 | tf_op jit(solution)/shard_map/ppermute | solution.py:323
  58.3 3.2 %collective-permute-done.17 = bf16[128,1408]{1,0:T(8,128)(2,1)S(1)} collective-permute-done((bf16[128,1408]{1,0:T(8,128)(2,1)S(1)}, bf16[128,1408]{1,0:T(8,128)(2,1)S(1)}, u32[]{:S(2)}, u32[]{:S(2)}) %collective-permute-start.17) | collective-permute-done | bytes 360480 | tf_op jit(solution)/shard_map/ppermute | solution.py:323
  62.8 3.3 %collective-permute-done.15.refs_8_.refs_10_ = bf16[2,128,1024]{2,1,0:T(8,128)(2,1)S(1)} collective-permute-done((bf16[2,128,1024]{2,1,0:T(8,128)(2,1)S(1)}, bf16[2,128,1024]{2,1,0:T(8,128)(2,1)S(1)}, u32[]{:S(2)}, u32[]{:S(2)}) %collective-permute-start.15) | collective-permute-done | bytes 524320 | tf_op jit(solution)/shard_map/ppermute | solution.py:323
  66.2 1.8 %collective-permute-start.8 = (bf16[2,128,1024]{2,1,0:T(8,128)(2,1)S(1)}, bf16[2,128,1024]{2,1,0:T(8,128)(2,1)S(1)}, u32[]{:S(2)}, u32[]{:S(2)}) collective-permute-start(bf16[2,128,1024]{2,1,0:T(8,128)(2,1)S(1)} %collective-permute-done.4.refs_2_), channel_id=1, source_target_pairs={{0,1},{1,0},{2,3},{3,2},{4,5},{5,4},{6,7},{7,6},{8,9},{9,8},{10,11... | collective-permute-start | bytes 1572872 | tf_op jit(solution)/shard_map/ppermute | solution.py:323
  68.0 4.6 %collective-permute-done.14.refs_8_.refs_9_ = bf16[2,128,1024]{2,1,0:T(8,128)(2,1)S(1)} collective-permute-done((bf16[2,128,1024]{2,1,0:T(8,128)(2,1)S(1)}, bf16[2,128,1024]{2,1,0:T(8,128)(2,1)S(1)}, u32[]{:S(2)}, u32[]{:S(2)}) %collective-permute-start.14) | collective-permute-done | bytes 524320 | tf_op jit(solution)/shard_map/ppermute | solution.py:323
  72.6 1.7 %collective-permute-start.22 = (bf16[128,1408]{1,0:T(8,128)(2,1)S(1)}, bf16[128,1408]{1,0:T(8,128)(2,1)S(1)}, u32[]{:S(2)}, u32[]{:S(2)}) collective-permute-start(bf16[128,1408]{1,0:T(8,128)(2,1)S(1)} %add_add_fusion.1), channel_id=1, source_target_pairs={{0,4},{32,36},{96,100},{64,68},{8,12},{40,44},{104,108},{72,76},{2... | collective-permute-start | bytes 1081352 | tf_op jit(solution)/shard_map/ppermute | solution.py:323
  74.3 1.3 %collective-permute-start.21 = (bf16[128,1408]{1,0:T(8,128)(2,1)S(1)}, bf16[128,1408]{1,0:T(8,128)(2,1)S(1)}, u32[]{:S(2)}, u32[]{:S(2)}) collective-permute-start(bf16[128,1408]{1,0:T(8,128)(2,1)S(1)} %add_add_fusion.1), channel_id=1, source_target_pairs={{0,6},{32,38},{96,102},{64,70},{8,14},{40,46},{104,110},{72,78},{2... | collective-permute-start | bytes 1081352 | tf_op jit(solution)/shard_map/ppermute | solution.py:323
  75.6 1.5 %collective-permute-start.20 = (bf16[128,1408]{1,0:T(8,128)(2,1)S(1)}, bf16[128,1408]{1,0:T(8,128)(2,1)S(1)}, u32[]{:S(2)}, u32[]{:S(2)}) collective-permute-start(bf16[128,1408]{1,0:T(8,128)(2,1)S(1)} %add_add_fusion.1), channel_id=1, source_target_pairs={{0,2},{32,34},{96,98},{64,66},{8,10},{40,42},{104,106},{72,74},{24... | collective-permute-start | bytes 1081352 | tf_op jit(solution)/shard_map/ppermute | solution.py:323
  85.2 14.8 %shard_map.33 = f32[2048,8,128]{2,1,0:T(8,128)} custom-call(s32[2]{0:T(128)S(1)} %pad_add_fusion.at_ref, bf16[2,128,1024]{2,1,0:T(8,128)(2,1)S(1)} %pad_maximum_fusion.refs_0_, bf16[2,128,1024]{2,1,0:T(8,128)(2,1)S(1)} %collective-permute-done.3.refs_1_, bf16[2,128,1024]{2,1,0:T(8,128)(2,1)S(1)} %collective-permute-done.4.refs_2_, ...), custom_call_target="tpu_custom_call" | custom-call | tf_op jit(solution)/shard_map/pallas_call | solution.py:297
  (42 shorter events, 16.9 us)
Async XLA Ops:
  0.0 9.6 %collective-permute-start = (bf16[128,1024]{1,0:T(8,128)(2,1)}, bf16[128,1024]{1,0:T(8,128)(2,1)S(1)}, u32[]{:S(2)}, u32[]{:S(2)}) collective-permute-start(bf16[128,1024]{1,0:T(8,128)(2,1)} %bitcast.7), channel_id=1, source_target_pairs={{0,8},{1,9},{2,10},{3,11},{4,12},{5,13},{6,14},{7,15},{8,0},{9,1},... | collective-permute-start | bytes 786440 | tf_op jit(solution)/shard_map/ppermute | solution.py:323
  2.5 9.7 %collective-permute-start.1 = (bf16[128,1024]{1,0:T(8,128)(2,1)}, bf16[128,1024]{1,0:T(8,128)(2,1)S(1)}, u32[]{:S(2)}, u32[]{:S(2)}) collective-permute-start(bf16[128,1024]{1,0:T(8,128)(2,1)} %bitcast.8), channel_id=1, source_target_pairs={{0,1},{1,0},{2,3},{3,2},{4,5},{5,4},{6,7},{7,6},{8,9},{9,8},{10,11... | collective-permute-start | bytes 786440 | tf_op jit(solution)/shard_map/ppermute | solution.py:323
  3.4 20.8 %collective-permute-start.2 = (bf16[128,1024]{1,0:T(8,128)(2,1)}, bf16[128,1024]{1,0:T(8,128)(2,1)S(1)}, u32[]{:S(2)}, u32[]{:S(2)}) collective-permute-start(bf16[128,1024]{1,0:T(8,128)(2,1)} %bitcast.9), channel_id=1, source_target_pairs={{0,0},{1,16},{2,8},{3,24},{4,32},{5,48},{6,40},{7,56},{8,64},{9,80... | collective-permute-start | bytes 786440 | tf_op jit(solution)/shard_map/ppermute | solution.py:323
  10.6 13.6 %collective-permute-start.4 = (bf16[2,128,1024]{2,1,0:T(8,128)(2,1)S(1)}, bf16[2,128,1024]{2,1,0:T(8,128)(2,1)S(1)}, u32[]{:S(2)}, u32[]{:S(2)}) collective-permute-start(bf16[2,128,1024]{2,1,0:T(8,128)(2,1)S(1)} %pad_maximum_fusion.refs_0_), channel_id=1, source_target_pairs={{0,6},{1,7},{2,0},{3,1},{4,2},{5,3},{6,4},{7,5},{8,14},{9,15},{10,... | collective-permute-start | bytes 1572872 | tf_op jit(solution)/shard_map/ppermute | solution.py:323
  12.1 20.5 %collective-permute-start.3 = (bf16[2,128,1024]{2,1,0:T(8,128)(2,1)S(1)}, bf16[2,128,1024]{2,1,0:T(8,128)(2,1)S(1)}, u32[]{:S(2)}, u32[]{:S(2)}) collective-permute-start(bf16[2,128,1024]{2,1,0:T(8,128)(2,1)S(1)} %pad_maximum_fusion.refs_0_), channel_id=1, source_target_pairs={{0,2},{1,3},{2,4},{3,5},{4,6},{5,7},{6,0},{7,1},{8,10},{9,11},{10,... | collective-permute-start | bytes 1572872 | tf_op jit(solution)/shard_map/ppermute | solution.py:323
  32.6 9.6 %collective-permute-start.13 = (bf16[128,1024]{1,0:T(8,128)(2,1)S(1)}, bf16[128,1024]{1,0:T(8,128)(2,1)S(1)}, u32[]{:S(2)}, u32[]{:S(2)}) collective-permute-start(bf16[128,1024]{1,0:T(8,128)(2,1)S(1)} %collective-permute-done.2), channel_id=1, source_target_pairs={{0,16},{1,17},{2,18},{3,19},{4,20},{5,21},{6,22},{7,23},{8,24},{9,... | collective-permute-start | bytes 786440 | tf_op jit(solution)/shard_map/ppermute | solution.py:323
  34.9 10.0 %collective-permute-start.12 = (bf16[128,1408]{1,0:T(8,128)(2,1)S(1)}, bf16[128,1408]{1,0:T(8,128)(2,1)S(1)}, u32[]{:S(2)}, u32[]{:S(2)}) collective-permute-start(bf16[128,1408]{1,0:T(8,128)(2,1)S(1)} %get-tuple-element.18), channel_id=1, source_target_pairs={{0,64},{1,17}} | collective-permute-start | bytes 1081352 | tf_op jit(solution)/shard_map/ppermute | solution.py:323
  37.5 9.1 %collective-permute-start.11 = (bf16[128,1408]{1,0:T(8,128)(2,1)S(1)}, bf16[128,1408]{1,0:T(8,128)(2,1)S(1)}, u32[]{:S(2)}, u32[]{:S(2)}) collective-permute-start(bf16[128,1408]{1,0:T(8,128)(2,1)S(1)} %get-tuple-element.18), channel_id=1, source_target_pairs={{0,96},{1,25}} | collective-permute-start | bytes 1081352 | tf_op jit(solution)/shard_map/ppermute | solution.py:323
  39.4 9.4 %collective-permute-start.10 = (bf16[128,1408]{1,0:T(8,128)(2,1)S(1)}, bf16[128,1408]{1,0:T(8,128)(2,1)S(1)}, u32[]{:S(2)}, u32[]{:S(2)}) collective-permute-start(bf16[128,1408]{1,0:T(8,128)(2,1)S(1)} %get-tuple-element.18), channel_id=1, source_target_pairs={{0,32},{1,9}} | collective-permute-start | bytes 1081352 | tf_op jit(solution)/shard_map/ppermute | solution.py:323
  40.7 15.2 %collective-permute-start.5 = (bf16[2,128,1024]{2,1,0:T(8,128)(2,1)S(1)}, bf16[2,128,1024]{2,1,0:T(8,128)(2,1)S(1)}, u32[]{:S(2)}, u32[]{:S(2)}) collective-permute-start(bf16[2,128,1024]{2,1,0:T(8,128)(2,1)S(1)} %pad_maximum_fusion.refs_0_), channel_id=1, source_target_pairs={{0,4},{1,5},{2,6},{3,7},{4,0},{5,1},{6,2},{7,3},{8,12},{9,13},{10,... | collective-permute-start | bytes 1572872 | tf_op jit(solution)/shard_map/ppermute | solution.py:323
  48.8 14.0 %collective-permute-start.16 = (bf16[2,128,1024]{2,1,0:T(8,128)(2,1)S(1)}, bf16[2,128,1024]{2,1,0:T(8,128)(2,1)S(1)}, u32[]{:S(2)}, u32[]{:S(2)}) collective-permute-start(bf16[2,128,1024]{2,1,0:T(8,128)(2,1)S(1)} %pad_maximum_fusion.1.refs_8_), channel_id=1, source_target_pairs={{0,64},{1,65},{2,66},{3,67},{4,68},{5,69},{6,70},{7,71},{8,72},{9,... | collective-permute-start | bytes 1572872 | tf_op jit(solution)/shard_map/ppermute | solution.py:323
  48.9 17.2 %collective-permute-start.15 = (bf16[2,128,1024]{2,1,0:T(8,128)(2,1)S(1)}, bf16[2,128,1024]{2,1,0:T(8,128)(2,1)S(1)}, u32[]{:S(2)}, u32[]{:S(2)}) collective-permute-start(bf16[2,128,1024]{2,1,0:T(8,128)(2,1)S(1)} %pad_maximum_fusion.1.refs_8_), channel_id=1, source_target_pairs={{0,96},{1,97},{2,98},{3,99},{4,100},{5,101},{6,102},{7,103},{8,104... | collective-permute-start | bytes 1572872 | tf_op jit(solution)/shard_map/ppermute | solution.py:323
  49.0 8.2 %collective-permute-start.19 = (bf16[128,1408]{1,0:T(8,128)(2,1)S(1)}, bf16[128,1408]{1,0:T(8,128)(2,1)S(1)}, u32[]{:S(2)}, u32[]{:S(2)}) collective-permute-start(bf16[128,1408]{1,0:T(8,128)(2,1)S(1)} %add_add_fusion.2), channel_id=1, source_target_pairs={{0,16},{32,48},{96,112},{64,80},{1,5},{9,13},{25,29},{17,21}} | collective-permute-start | bytes 1081352 | tf_op jit(solution)/shard_map/ppermute | solution.py:323
  50.3 7.0 %collective-permute-start.18 = (bf16[128,1408]{1,0:T(8,128)(2,1)S(1)}, bf16[128,1408]{1,0:T(8,128)(2,1)S(1)}, u32[]{:S(2)}, u32[]{:S(2)}) collective-permute-start(bf16[128,1408]{1,0:T(8,128)(2,1)S(1)} %add_add_fusion.2), channel_id=1, source_target_pairs={{0,24},{32,56},{96,120},{64,88},{1,7},{9,15},{25,31},{17,23}} | collective-permute-start | bytes 1081352 | tf_op jit(solution)/shard_map/ppermute | solution.py:323
  55.9 5.6 %collective-permute-start.17 = (bf16[128,1408]{1,0:T(8,128)(2,1)S(1)}, bf16[128,1408]{1,0:T(8,128)(2,1)S(1)}, u32[]{:S(2)}, u32[]{:S(2)}) collective-permute-start(bf16[128,1408]{1,0:T(8,128)(2,1)S(1)} %add_add_fusion.2), channel_id=1, source_target_pairs={{0,8},{32,40},{96,104},{64,72},{1,3},{9,11},{25,27},{17,19}} | collective-permute-start | bytes 1081352 | tf_op jit(solution)/shard_map/ppermute | solution.py:323
  57.2 15.4 %collective-permute-start.14 = (bf16[2,128,1024]{2,1,0:T(8,128)(2,1)S(1)}, bf16[2,128,1024]{2,1,0:T(8,128)(2,1)S(1)}, u32[]{:S(2)}, u32[]{:S(2)}) collective-permute-start(bf16[2,128,1024]{2,1,0:T(8,128)(2,1)S(1)} %pad_maximum_fusion.1.refs_8_), channel_id=1, source_target_pairs={{0,32},{1,33},{2,34},{3,35},{4,36},{5,37},{6,38},{7,39},{8,40},{9,... | collective-permute-start | bytes 1572872 | tf_op jit(solution)/shard_map/ppermute | solution.py:323
  57.3 17.0 %collective-permute-start.6 = (bf16[2,128,1024]{2,1,0:T(8,128)(2,1)S(1)}, bf16[2,128,1024]{2,1,0:T(8,128)(2,1)S(1)}, u32[]{:S(2)}, u32[]{:S(2)}) collective-permute-start(bf16[2,128,1024]{2,1,0:T(8,128)(2,1)S(1)} %pad_maximum_fusion.refs_0_), channel_id=1, source_target_pairs={{0,1},{1,0},{2,3},{3,2},{4,5},{5,4},{6,7},{7,6},{8,9},{9,8},{10,11... | collective-permute-start | bytes 1572872 | tf_op jit(solution)/shard_map/ppermute | solution.py:323
  61.5 15.6 %collective-permute-start.7 = (bf16[2,128,1024]{2,1,0:T(8,128)(2,1)S(1)}, bf16[2,128,1024]{2,1,0:T(8,128)(2,1)S(1)}, u32[]{:S(2)}, u32[]{:S(2)}) collective-permute-start(bf16[2,128,1024]{2,1,0:T(8,128)(2,1)S(1)} %collective-permute-done.3.refs_1_), channel_id=1, source_target_pairs={{0,1},{1,0},{2,3},{3,2},{4,5},{5,4},{6,7},{7,6},{8,9},{9,8},{10,11... | collective-permute-start | bytes 1572872 | tf_op jit(solution)/shard_map/ppermute | solution.py:323
  62.8 12.8 %collective-permute-start.9 = (bf16[2,128,1024]{2,1,0:T(8,128)(2,1)S(1)}, bf16[2,128,1024]{2,1,0:T(8,128)(2,1)S(1)}, u32[]{:S(2)}, u32[]{:S(2)}) collective-permute-start(bf16[2,128,1024]{2,1,0:T(8,128)(2,1)S(1)} %collective-permute-done.5.refs_3_), channel_id=1, source_target_pairs={{0,1},{1,0},{2,3},{3,2},{4,5},{5,4},{6,7},{7,6},{8,9},{9,8},{10,11... | collective-permute-start | bytes 1572872 | tf_op jit(solution)/shard_map/ppermute | solution.py:323
  66.2 11.0 %collective-permute-start.8 = (bf16[2,128,1024]{2,1,0:T(8,128)(2,1)S(1)}, bf16[2,128,1024]{2,1,0:T(8,128)(2,1)S(1)}, u32[]{:S(2)}, u32[]{:S(2)}) collective-permute-start(bf16[2,128,1024]{2,1,0:T(8,128)(2,1)S(1)} %collective-permute-done.4.refs_2_), channel_id=1, source_target_pairs={{0,1},{1,0},{2,3},{3,2},{4,5},{5,4},{6,7},{7,6},{8,9},{9,8},{10,11... | collective-permute-start | bytes 1572872 | tf_op jit(solution)/shard_map/ppermute | solution.py:323
  72.6 9.7 %collective-permute-start.22 = (bf16[128,1408]{1,0:T(8,128)(2,1)S(1)}, bf16[128,1408]{1,0:T(8,128)(2,1)S(1)}, u32[]{:S(2)}, u32[]{:S(2)}) collective-permute-start(bf16[128,1408]{1,0:T(8,128)(2,1)S(1)} %add_add_fusion.1), channel_id=1, source_target_pairs={{0,4},{32,36},{96,100},{64,68},{8,12},{40,44},{104,108},{72,76},{2... | collective-permute-start | bytes 1081352 | tf_op jit(solution)/shard_map/ppermute | solution.py:323
  74.3 8.0 %collective-permute-start.21 = (bf16[128,1408]{1,0:T(8,128)(2,1)S(1)}, bf16[128,1408]{1,0:T(8,128)(2,1)S(1)}, u32[]{:S(2)}, u32[]{:S(2)}) collective-permute-start(bf16[128,1408]{1,0:T(8,128)(2,1)S(1)} %add_add_fusion.1), channel_id=1, source_target_pairs={{0,6},{32,38},{96,102},{64,70},{8,14},{40,46},{104,110},{72,78},{2... | collective-permute-start | bytes 1081352 | tf_op jit(solution)/shard_map/ppermute | solution.py:323
  75.6 6.9 %collective-permute-start.20 = (bf16[128,1408]{1,0:T(8,128)(2,1)S(1)}, bf16[128,1408]{1,0:T(8,128)(2,1)S(1)}, u32[]{:S(2)}, u32[]{:S(2)}) collective-permute-start(bf16[128,1408]{1,0:T(8,128)(2,1)S(1)} %add_add_fusion.1), channel_id=1, source_target_pairs={{0,2},{32,34},{96,98},{64,66},{8,10},{40,42},{104,106},{72,74},{24... | collective-permute-start | bytes 1081352 | tf_op jit(solution)/shard_map/ppermute | solution.py:323
  82.6 2.6 %collective-permute-start.23 = (bf16[128,1408]{1,0:T(8,128)(2,1)S(1)}, bf16[128,1408]{1,0:T(8,128)(2,1)S(1)}, u32[]{:S(2)}, u32[]{:S(2)}) collective-permute-start(bf16[128,1408]{1,0:T(8,128)(2,1)S(1)} %add_add_fusion.refs_16_), channel_id=1, source_target_pairs={{0,1},{1,0},{2,3},{3,2},{4,5},{5,4},{6,7},{7,6},{8,9},{9,8},{10,11... | collective-permute-start | bytes 1081352 | tf_op jit(solution)/shard_map/ppermute | solution.py:323
  (3 other events, 5.8 us)
